TPU v7x, 512 devices: a whole 4x8x8 slice. The times are simulated.
512 devices in a mesh: grp: 8 (over x, core), seg: 64 (over z, y).
Axes of the slice: x: 4, y: 8, z: 8, core: 2. Of those that a mesh axis runs over, the one named last changes fastest.
Arguments:
- positions: float32 [3, 2097152], P(None, ('grp', 'seg')), may hold values from -18 to 18
- normals: float32 [3, 2097152], P(None, ('grp', 'seg')), may hold values from -3 to 3
- scales: float32 [2097152], P(('grp', 'seg')), may hold values from 0.5 to 2
- displacement: float32 [3, 2097152], P(None, ('grp', 'seg')), may hold values from -6 to 6
- pair_list: int32 [2, 81920], P(None, ('grp', 'seg')), may hold values from 0 to 63, as said below
- pair_count: int32 [512], P(('grp', 'seg')), may hold values from 32 to 160, as said below
- base_aperture: float32 [2097152], P(('grp', 'seg')), may hold values from 0.5 to 1.2
- storage: float32 [2097152], P(('grp', 'seg')), may hold values from 0.5 to 2
- injection: float32 [2097152], P(('grp', 'seg')), may hold values from -6 to 6
- link_offset: int32 [2097152], P(('grp', 'seg')), may hold values from 1 to 4096
Outputs:
- traction: float32 [3, 2097152], P(None, ('grp', 'seg'))
- pressure: float32 [2097152], P(('grp', 'seg'))
- residual: float32 [2097152], P(('grp', 'seg'))
Inputs may be any that keep to these rules, and one draw needn't show every extreme that they name: `pair_list`: in each device's 160 slots, the first 32 pairs are (t, t + 32) for t = 0 to 31; every other used pair (t, s) has t + 1 <= s + 1 <= t + 32, i.e. s from t to t + 31; no used pair occurs twice; slots from pair_count on hold (0, 32) and are unused. `pair_count`: some device uses all 160 slots.
All inputs are finite; a program needn't handle non-finite values.
Results may differ from a plain program's by a relative error of at most 0.0003.
Values sent between devices are 32-bit elements; how exact they have to be, the bound alone decides.
A program may use at most 64 MiB of HBM per device.

v0:
```python
import jax
import jax.numpy as jnp
from jax import lax
from jax.sharding import PartitionSpec as P

BLK = 128
ITERS = 2
NB = 32


pairs_per_step = 16


def from_behind(block, axis, distance):
    devices = range(lax.axis_size(axis))
    route = [(i - distance, i) for i in devices if i - distance in devices]
    return lax.ppermute(block, axis, route)


def tiles(tpos, tnrm, tscl, spos, snrm, sscl):
    dist = jnp.zeros(tscl.shape + (sscl.shape[-1],), jnp.float32)
    align = jnp.zeros(tscl.shape + (sscl.shape[-1],), jnp.float32)
    for comp in range(3):
        diff = tpos[comp][:, :, None] - spos[comp][:, None, :]
        dist = dist + diff * diff
        align = align + tnrm[comp][:, :, None] * snrm[comp][:, None, :]
    return 0.25 * tscl[:, :, None] * sscl[:, None, :] * (1.0 + 0.5 * align) / jnp.sqrt(0.25 + dist)


def sweep(frame, pairs, count, low, high):
    pos, nrm, scl, dsp = frame
    slots = pairs.shape[1]
    steps = (count + pairs_per_step - 1) // pairs_per_step

    def one(group, acc):
        slot = group * pairs_per_step + jnp.arange(pairs_per_step, dtype=jnp.int32)
        live = slot < count
        slot = jnp.minimum(slot, slots - 1)
        tgt = pairs[0, slot] + NB
        src = pairs[1, slot]
        kern = tiles(pos[:, tgt], nrm[:, tgt], scl[tgt], pos[:, src], nrm[:, src], scl[src])
        keep = live & (src != tgt) & (src >= low) & (src < high)
        bck = jnp.einsum("gab,cga->cgb", kern, dsp[:, tgt], precision=lax.Precision.HIGHEST)
        acc = acc.at[:, src].add(bck * keep.astype(jnp.float32)[None, :, None])
        fwd = jnp.einsum("gab,cgb->cga", kern, dsp[:, src], precision=lax.Precision.HIGHEST)
        acc = acc.at[:, tgt].add(fwd * live.astype(jnp.float32)[None, :, None])
        return acc

    return lax.fori_loop(0, steps, one, jnp.zeros(dsp.shape, jnp.float32))


def make_frame(first, second):
    pos = jnp.concatenate([first[0], second[0]], 1).reshape(3, 2 * NB, BLK)
    nrm = jnp.concatenate([first[1], second[1]], 1).reshape(3, 2 * NB, BLK)
    scl = jnp.concatenate([first[2], second[2]], 0).reshape(2 * NB, BLK)
    dsp = jnp.concatenate([first[3], second[3]], 1).reshape(3, 2 * NB, BLK)
    return (pos, nrm, scl, dsp)


def flow_apply(vec, weight, target, storage):
    count = vec.shape[0]
    after = from_behind(vec, ("grp", "seg"), -1)
    flux = weight * (vec - jnp.concatenate([vec, after])[target])
    landed = jnp.zeros((2 * count,), jnp.float32).at[target].add(-flux)
    arrived = from_behind(landed[count:], ("grp", "seg"), 1)
    return storage * vec + flux + landed[:count] + arrived


def residual_squares(vec):
    return lax.psum(jnp.sum(vec * vec), ("grp", "seg"))


def shards(
    positions,
    normals,
    scales,
    displacement,
    pair_list,
    pair_count,
    base_aperture,
    storage,
    injection,
    link_offset,
):
    count_el = positions.shape[1]
    own = (positions, normals, scales, displacement)
    prior = from_behind((positions, normals, scales, displacement), ("grp", "seg"), 1)
    frame = make_frame(prior, own)
    acc = sweep(frame, pair_list, pair_count[0], 0, 2 * NB)
    returned = from_behind(acc[:, :NB], ("grp", "seg"), -1)
    traction = (acc[:, NB:] + returned).reshape(3, count_el)
    aperture = base_aperture * (1.0 + 0.5 * jnp.tanh(traction[0]))
    cube = aperture * aperture * aperture
    cube_after = from_behind(cube, ("grp", "seg"), -1)
    local = jnp.arange(count_el, dtype=jnp.int32)
    target = local + link_offset
    total = lax.axis_size(("grp", "seg")) * count_el
    inside = (lax.axis_index(("grp", "seg")) * count_el + target < total).astype(jnp.float32)
    weight = 0.5 * (cube + jnp.concatenate([cube, cube_after])[target]) * inside
    pressure = jnp.zeros_like(injection)
    residual = injection
    direction = injection
    norm_now = residual_squares(residual)
    for it in range(ITERS):
        image = flow_apply(direction, weight, target, storage)
        alpha = norm_now / lax.psum(jnp.sum(direction * image), ("grp", "seg"))
        pressure = pressure + alpha * direction
        residual = residual - alpha * image
        norm_next = residual_squares(residual)
        direction = residual + norm_next / norm_now * direction
        norm_now = norm_next
    return (traction, pressure, residual)


def solution(mesh):
    return jax.shard_map(
        shards,
        mesh=mesh,
        in_specs=(
            P(None, ("grp", "seg")),
            P(None, ("grp", "seg")),
            P(("grp", "seg")),
            P(None, ("grp", "seg")),
            P(None, ("grp", "seg")),
            P(("grp", "seg")),
            P(("grp", "seg")),
            P(("grp", "seg")),
            P(("grp", "seg")),
            P(("grp", "seg")),
        ),
        out_specs=(P(None, ("grp", "seg")), P(("grp", "seg")), P(("grp", "seg"))),
        check_vma=False,
    )
```

profile of v0, /device:TPU:1, one launch (start us, length us, event | category | flops | bytes accessed | tf_op | source)
XLA Modules:
  0.0 629.2 jit_solution(14374003382576178828)
XLA Ops:
  0.6 4.2 collective-permute-start.1
  4.8 3.2 collective-permute-start
  8.0 3.2 collective-permute-start.2
  11.2 4.4 collective-permute-start.3
  15.7 7.8 %collective-permute-start.6 = (f32[4096]{0:T(1024)}, f32[4096]{0:T(1024)S(1)}, u32[]{:S(2)}, u32[]{:S(2)}) collective-permute-start(f32[4096]{0:T(1024)} %param.20), channel_id=1, source_target_pairs={{1,0},{2,1},{3,2},{4,3},{5,4},{6,5},{7,6},{8,7},{9,8},{10,9},{11,1... | collective-permute-start | bytes 49160 | tf_op jit(solution)/shard_map/ppermute | solution.py:17
  24.1 0.7 pad_maximum_fusion
  24.9 0.8 copy-done.6
  25.8 0.6 copy-done
  26.5 49.6 %while.12 = (s32[]{:T(128)}, f32[3,64,128]{2,0,1:T(4,128)S(1)}, s32[]{:T(128)}, s32[2,160]{1,0:T(2,128)S(1)}, f32[3,64,128]{2,0,1:T(4,128)S(1)}, /*index=5*/f32[...) while((s32[]{:T(128)}, f32[3,64,128]{2,0,1:T(4,128)S(1)}, ...), condition=%wide.region_3.4_spmd, body=%wide.region_0.3_spmd.sunk | while | flops 28865044 | bytes 1026185 | solution.py:49
  26.5 0.7 gather_fusion
  27.2 0.7 gather_fusion.2
  27.9 0.7 and_convert_fusion.2
  28.6 0.6 gather_fusion.1
  29.2 0.6 gather_fusion.3
  30.5 0.6 gather_fusion.5
  32.2 0.6 gather_fusion.9
  32.8 4.0 convolution_multiply_fusion.5
  36.8 0.6 gather_fusion.8
  37.4 3.3 convolution_multiply_fusion.4
  40.8 1.1 scatter_fusion
  41.9 1.1 scatter_fusion.1
  43.0 0.7 gather_fusion
  43.7 0.7 gather_fusion.2
  44.4 0.7 and_convert_fusion.2
  45.7 0.6 gather_fusion.3
  46.4 0.6 gather_fusion.4
  49.3 4.0 convolution_multiply_fusion.5
  53.3 0.6 gather_fusion.8
  53.9 3.3 convolution_multiply_fusion.4
  57.3 1.1 scatter_fusion
  58.4 1.1 scatter_fusion.1
  59.5 0.7 gather_fusion
  60.2 0.7 gather_fusion.2
  60.9 0.7 and_convert_fusion.2
  61.6 0.6 gather_fusion.1
  62.3 0.6 gather_fusion.3
  65.2 0.6 gather_fusion.9
  65.8 4.0 convolution_multiply_fusion.5
  69.8 0.6 gather_fusion.8
  70.4 3.4 convolution_multiply_fusion.4
  73.8 1.1 scatter_fusion
  74.9 1.1 scatter_fusion.1
  76.1 70.0 %collective-permute-start.4 = (f32[3,32,128]{2,0,1:T(4,128)S(1)}, f32[3,32,128]{2,0,1:T(4,128)S(1)}, u32[]{:S(2)}, u32[]{:S(2)}) collective-permute-start(f32[3,32,128]{2,0,1:T(4,128)S(1)} %slice.95), channel_id=1, source_target_pairs={{1,0},{2,1},{3,2},{4,3},{5,4},{6,5},{7,6},{8,7},{9,8},{10,9},{11,1... | collective-permute-start | bytes 147464 | tf_op jit(solution)/shard_map/ppermute | solution.py:17
  146.1 11.8 %collective-permute-done.4 = f32[3,32,128]{2,0,1:T(4,128)S(1)} collective-permute-done((f32[3,32,128]{2,0,1:T(4,128)S(1)}, f32[3,32,128]{2,0,1:T(4,128)S(1)}, u32[]{:S(2)}, u32[]{:S(2)}) %collective-permute-start.4) | collective-permute-done | bytes 49184 | tf_op jit(solution)/shard_map/ppermute | solution.py:17
  158.0 0.7 copy-done.8
  158.7 2.0 collective-permute-start.5
  160.8 23.0 %gather_fusion.11 = f32[4096]{0:T(1024)S(1)} fusion(f32[8192]{0:T(1024)S(1)} %pad_maximum_fusion.2, s32[4096]{0:T(1024)S(1)} %get-tuple-element.162), kind=kCustom, calls=%fused_computation.11 | custom fusion | bytes 49152 | tf_op jit(solution)/shard_map/gather | solution.py:63
  183.9 23.0 %gather_fusion.10 = f32[4096]{0:T(1024)S(1)} fusion(f32[8192]{0:T(1024)S(1)} %pad_maximum_fusion.1, s32[4096]{0:T(1024)S(1)} %get-tuple-element.162), kind=kCustom, calls=%fused_computation.10 | custom fusion | bytes 49152 | tf_op jit(solution)/shard_map/gather | solution.py:99
  206.9 21.9 %scatter_custom_fusion.2 = f32[8192]{0:T(1024)S(1)} fusion(s32[4096]{0:T(1024)S(1)} %get-tuple-element.163, f32[4096]{0:T(1024)S(1)} %get-tuple-element.144, f32[]{:T(128)} %constant.91.clone.1), kind=kCustom, calls=%fused_computation.70 | custom fusion | flops 4096 | bytes 32772 | tf_op jit(solution)/shard_map/scatter-add | solution.py:64
  228.9 3.4 collective-permute-start.7
  232.3 10.6 %collective-permute-done.7 = f32[4096]{0:T(1024)S(1)} collective-permute-done((f32[4096]{0:T(1024)S(1)}, f32[4096]{0:T(1024)S(1)}, u32[]{:S(2)}, u32[]{:S(2)}) %collective-permute-start.7) | collective-permute-done | bytes 16416 | tf_op jit(solution)/shard_map/ppermute | solution.py:17
  242.8 0.6 multiply_reduce_fusion.2
  243.4 133.4 %all-reduce.2 = (f32[]{:T(128)}, f32[]{:T(128)}) all-reduce(f32[]{:T(128)} %get-tuple-element.121, f32[]{:T(128)} %get-tuple-element.120), channel_id=1, replica_groups=mesh['grp'=8,'seg'=64] {'grp','seg'}, use_global_device_ids=true, to_apply=%region_5.6 | all-reduce | flops 2 | bytes 16 | tf_op jit(solution)/shard_map/psum | solution.py:70
  378.2 0.6 multiply_reduce_fusion.1
  378.8 94.4 %psum.30 = f32[]{:T(128)} all-reduce(f32[]{:T(128)} %get-tuple-element.142), channel_id=1, replica_groups=mesh['grp'=8,'seg'=64] {'grp','seg'}, use_global_device_ids=true, to_apply=%region_10.11 | all-reduce | flops 1 | bytes 8 | tf_op jit(solution)/shard_map/psum | solution.py:70
  474.5 3.6 collective-permute-start.8
  478.2 0.8 collective-permute-done.8
  479.0 23.0 %gather_fusion.12 = f32[4096]{0:T(1024)S(1)} fusion(f32[8192]{0:T(1024)S(1)} %pad_maximum_fusion.3, s32[4096]{0:T(1024)S(1)} %get-tuple-element.162), kind=kCustom, calls=%fused_computation.12 | custom fusion | bytes 49152 | tf_op jit(solution)/shard_map/gather | solution.py:63
  502.1 21.9 %scatter_custom_fusion.3 = f32[8192]{0:T(1024)S(1)} fusion(s32[4096]{0:T(1024)S(1)} %get-tuple-element.163, f32[4096]{0:T(1024)S(1)} %fusion.21, f32[]{:T(128)} %constant.91.clone.1), kind=kCustom, calls=%fused_computation.68 | custom fusion | flops 4096 | bytes 32772 | tf_op jit(solution)/shard_map/scatter-add | solution.py:64
  524.0 1.9 collective-permute-start.9
  525.9 7.0 %collective-permute-done.9 = f32[4096]{0:T(1024)S(1)} collective-permute-done((f32[4096]{0:T(1024)S(1)}, f32[4096]{0:T(1024)S(1)}, u32[]{:S(2)}, u32[]{:S(2)}) %collective-permute-start.9) | collective-permute-done | bytes 16416 | tf_op jit(solution)/shard_map/ppermute | solution.py:17
  533.0 0.6 multiply_reduce_fusion
  533.6 93.6 %psum.31 = f32[]{:T(128)} all-reduce(f32[]{:T(128)} %multiply_reduce_fusion), channel_id=1, replica_groups=mesh['grp'=8,'seg'=64] {'grp','seg'}, use_global_device_ids=true, to_apply=%region_13.14 | all-reduce | flops 1 | bytes 8 | tf_op jit(solution)/shard_map/psum | solution.py:106
  628.5 0.6 multiply_subtract_fusion
  (83 shorter events, 7.6 us)
Async XLA Ops:
  0.6 24.2 %copy-start.5 = (f32[3,4096]{1,0:T(4,128)S(1)}, f32[3,4096]{1,0:T(4,128)}, u32[]{:S(2)}) copy-start(f32[3,4096]{1,0:T(4,128)} %param.15) | copy-start | bytes 147460
  0.6 23.5 %collective-permute-start.1 = (f32[4096]{0:T(1024)}, f32[4096]{0:T(1024)S(1)}, u32[]{:S(2)}, u32[]{:S(2)}) collective-permute-start(f32[4096]{0:T(1024)} %param.14), channel_id=1, source_target_pairs={{0,1},{1,2},{2,3},{3,4},{4,5},{5,6},{6,7},{7,8},{8,9},{9,10},{10,1... | collective-permute-start | bytes 49160 | tf_op jit(solution)/shard_map/ppermute | solution.py:17
  4.8 20.1 %collective-permute-start = (f32[3,4096]{1,0:T(4,128)}, f32[3,4096]{1,0:T(4,128)S(1)}, u32[]{:S(2)}, u32[]{:S(2)}) collective-permute-start(f32[3,4096]{1,0:T(4,128)} %param.15), channel_id=1, source_target_pairs={{0,1},{1,2},{2,3},{3,4},{4,5},{5,6},{6,7},{7,8},{8,9},{9,10},{10,1... | collective-permute-start | bytes 147464 | tf_op jit(solution)/shard_map/ppermute | solution.py:17
  8.0 16.9 %collective-permute-start.2 = (f32[3,4096]{1,0:T(4,128)}, f32[3,4096]{1,0:T(4,128)S(1)}, u32[]{:S(2)}, u32[]{:S(2)}) collective-permute-start(f32[3,4096]{1,0:T(4,128)} %param.13), channel_id=1, source_target_pairs={{0,1},{1,2},{2,3},{3,4},{4,5},{5,6},{6,7},{7,8},{8,9},{9,10},{10,1... | collective-permute-start | bytes 147464 | tf_op jit(solution)/shard_map/ppermute | solution.py:17
  11.2 14.5 %collective-permute-start.3 = (f32[3,4096]{1,0:T(4,128)}, f32[3,4096]{1,0:T(4,128)S(1)}, u32[]{:S(2)}, u32[]{:S(2)}) collective-permute-start(f32[3,4096]{1,0:T(4,128)} %param.12), channel_id=1, source_target_pairs={{0,1},{1,2},{2,3},{3,4},{4,5},{5,6},{6,7},{7,8},{8,9},{9,10},{10,1... | collective-permute-start | bytes 147464 | tf_op jit(solution)/shard_map/ppermute | solution.py:17
  15.7 145.1 %collective-permute-start.6 = (f32[4096]{0:T(1024)}, f32[4096]{0:T(1024)S(1)}, u32[]{:S(2)}, u32[]{:S(2)}) collective-permute-start(f32[4096]{0:T(1024)} %param.20), channel_id=1, source_target_pairs={{1,0},{2,1},{3,2},{4,3},{5,4},{6,5},{7,6},{8,7},{9,8},{10,9},{11,1... | collective-permute-start | bytes 49160 | tf_op jit(solution)/shard_map/ppermute | solution.py:17
  24.9 0.8 copy-start.6
  24.9 0.8 copy-start.7
  25.8 0.7 copy-start
  76.1 70.0 %copy-start.4 = (s32[4096]{0:T(1024)S(1)}, s32[4096]{0:T(1024)}, u32[]{:S(2)}) copy-start(s32[4096]{0:T(1024)} %param.21) | copy-start | bytes 49156
  76.1 81.8 %collective-permute-start.4 = (f32[3,32,128]{2,0,1:T(4,128)S(1)}, f32[3,32,128]{2,0,1:T(4,128)S(1)}, u32[]{:S(2)}, u32[]{:S(2)}) collective-permute-start(f32[3,32,128]{2,0,1:T(4,128)S(1)} %slice.95), channel_id=1, source_target_pairs={{1,0},{2,1},{3,2},{4,3},{5,4},{6,5},{7,6},{8,7},{9,8},{10,9},{11,1... | collective-permute-start | bytes 147464 | tf_op jit(solution)/shard_map/ppermute | solution.py:17
  158.0 2.9 copy-start.3
  158.0 0.7 copy-start.8
  158.7 2.1 copy-start.1
  158.7 25.1 %collective-permute-start.5 = (f32[4096]{0:T(1024)S(1)}, f32[4096]{0:T(1024)S(1)}, u32[]{:S(2)}, u32[]{:S(2)}) collective-permute-start(f32[4096]{0:T(1024)S(1)} %multiply_multiply_fusion), channel_id=1, source_target_pairs={{1,0},{2,1},{3,2},{4,3},{5,4},{6,5},{7,6},{8,7},{9,8},{10,9},{11,1... | collective-permute-start | bytes 49160 | tf_op jit(solution)/shard_map/ppermute | solution.py:17
  228.9 14.0 %copy-start.2 = (f32[4096]{0:T(1024)S(1)}, f32[4096]{0:T(1024)}, u32[]{:S(2)}) copy-start(f32[4096]{0:T(1024)} %param.19) | copy-start | bytes 49156
  228.9 13.9 %collective-permute-start.7 = (f32[4096]{0:T(1024)S(1)}, f32[4096]{0:T(1024)S(1)}, u32[]{:S(2)}, u32[]{:S(2)}) collective-permute-start(f32[4096]{0:T(1024)S(1)} %slice.141), channel_id=1, source_target_pairs={{0,1},{1,2},{2,3},{3,4},{4,5},{5,6},{6,7},{7,8},{8,9},{9,10},{10,1... | collective-permute-start | bytes 49160 | tf_op jit(solution)/shard_map/ppermute | solution.py:17
  474.5 4.5 collective-permute-start.8
  524.0 8.9 %collective-permute-start.9 = (f32[4096]{0:T(1024)S(1)}, f32[4096]{0:T(1024)S(1)}, u32[]{:S(2)}, u32[]{:S(2)}) collective-permute-start(f32[4096]{0:T(1024)S(1)} %slice.143), channel_id=1, source_target_pairs={{0,1},{1,2},{2,3},{3,4},{4,5},{5,6},{6,7},{7,8},{8,9},{9,10},{10,1... | collective-permute-start | bytes 49160 | tf_op jit(solution)/shard_map/ppermute | solution.py:17
where the time goes:
time: 630 us; the launch traced here: 629 us
  blocking collectives  321 us (51%)
  starting transfers between devices  104 us (17%)
  local copies, waits for them, and re-layouts  89.7 us (14%)
  other arithmetic  56 us (9%)
  waiting for transfers between devices  30.2 us (5%)
  matrix products  22.1 us (4%)
    psum x2, blocking collectives, residual_squares(): return lax.psum(jnp.sum(vec * vec), ('grp', 'seg'))  228 us
    ppermute x10, starting transfers between devices, from_behind(): return lax.ppermute(block, axis, route)  104 us
    psum x1, blocking collectives, shards(): alpha = norm_now / lax.psum(jnp.sum(direction * image), ('grp', 'seg'))  93.6 us
    gather x2, local copies, waits for them, and re-layouts, flow_apply(): flux = weight * (vec - jnp.concatenate([vec, after])[target])  46.1 us
    scatter-add x2, other arithmetic, flow_apply(): landed = jnp.zeros((2 * count,), jnp.float32).at[target].add(-flux)  43.9 us
    ppermute x10, waiting for transfers between devices, from_behind(): return lax.ppermute(block, axis, route)  30.2 us
    gather x1, local copies, waits for them, and re-layouts, shards(): weight = 0.5 * (cube + jnp.concatenate([cube, cube_after])[target]) * inside  23 us
  transfers between devices with their start and end apart: 10, of which 4 were waited for; matrix products, arithmetic and copies ran while one was open for 12% of the time, Pallas kernels for 0%

commit v1 on v0

v1 whole, which is shorter than its diff:
```python
import functools

import jax
import jax.numpy as jnp
from jax import lax
from jax.experimental import pallas as pl
from jax.experimental.pallas import tpu as pltpu
from jax.sharding import PartitionSpec as P

BLK = 128
NB = 32
PMAX = 160
F32 = jnp.float32
BF16 = jnp.bfloat16
MESH = pl.DeviceIdType.MESH
NT = (((1,), (1,)), ((), ()))
UNROLL = 8


def split(x, parts):
    out = []
    for _ in range(parts - 1):
        top = x.astype(BF16).astype(F32)
        out.append(top)
        x = x - top
    return out + [x]


def quads(vec, last):
    return jnp.concatenate([vec, last, vec, last], 0)


def kernel(
    grp_size,
    seg_size,
    low_size,
    pairs,
    count,
    pos,
    nrm,
    scl,
    dsp,
    pair_rows,
    base,
    sto,
    inj,
    off,
    traction,
    pressure,
    residual,
    prev_pos,
    prev_nrm,
    prev_scl,
    prev_dsp,
    base_next,
    table_inj,
    tfeat,
    sfeat,
    dfeat,
    held,
    con_t,
    con_s,
    near0,
    near12,
    got0,
    got0_far,
    got12,
    onehot,
    lanes_hot,
    rows_hot,
    spread,
    table,
    landed_out,
    landed_in,
    part_out,
    part_in,
    landed2_out,
    landed2_in,
    sums_out,
    sums_grp,
    sums_low,
    sums_high,
    send_sem,
    recv_sem,
    red_send,
    red_recv,
):
    devices = grp_size * seg_size
    high_size = seg_size // low_size
    grp = lax.axis_index("grp")
    seg = lax.axis_index("seg")
    me = grp * seg_size + seg

    def device(shift):
        to = lax.rem(me + shift + devices, devices)
        return (to // seg_size, lax.rem(to, seg_size))

    def grp_mate(j):
        return (lax.rem(grp + j, grp_size), seg)

    def low_mate(j):
        return (grp, seg // low_size * low_size + lax.rem(lax.rem(seg, low_size) + j, low_size))

    def high_mate(j):
        return (grp, lax.rem(seg + j * low_size, seg_size))

    mates = [device(shift) for shift in (1, -1, 2, -2)]
    mates += [grp_mate(j) for j in range(1, grp_size)]
    mates += [low_mate(j) for j in range(1, low_size)]
    mates += [high_mate(j) for j in range(1, high_size)]
    barrier = pltpu.get_barrier_semaphore()
    for mate in mates:
        pl.semaphore_signal(barrier, inc=1, device_id=mate, device_id_type=MESH)
    pl.semaphore_wait(barrier, len(mates))

    def send(src, dst, slot, to):
        copy = pltpu.make_async_remote_copy(
            src_ref=src,
            dst_ref=dst,
            send_sem=send_sem.at[slot],
            recv_sem=recv_sem.at[slot],
            device_id=to,
            device_id_type=MESH,
        )
        copy.start()
        return copy

    after, before, before2 = device(1), device(-1), device(-2)
    frame = [
        send(pos, prev_pos, 0, after),
        send(nrm, prev_nrm, 1, after),
        send(scl, prev_scl, 2, after),
        send(dsp, prev_dsp, 3, after),
    ]
    early = [
        send(base, base_next, 4, before),
        send(inj, table_inj.at[pl.ds(NB, NB)], 5, before),
    ]

    row = lax.broadcasted_iota(jnp.int32, (8, BLK), 0)
    low4 = row < 4
    is3 = row == 3
    is7 = row == 7
    is_norm = is3 | is7
    zeros8 = jnp.zeros((8, BLK), F32)
    centre = jnp.mean(pos[...], axis=1, keepdims=True)

    def target_block(k, _):
        lane = pl.ds(pl.multiple_of(k * BLK, BLK), BLK)
        p = pos[:, lane] - centre
        q = quads(p, jnp.sum(p * p, axis=0, keepdims=True))
        q1, q2, q3 = split(jnp.where(is_norm, q, -2.0 * q), 3)
        s = scl[pl.ds(k, 1), :]
        r = quads(nrm[:, lane] * s * 0.125, 0.25 * s)
        r1, r2, r3 = split(r, 3)
        rows = [
            jnp.where(is7, 1.0, q1),
            jnp.where(is7, 1.0, q2),
            jnp.where(is7, 1.0, jnp.where(low4, q3, q1)),
            r1,
            r2,
            jnp.where(low4, r3, r1),
        ]
        rows += [zeros8] * 10
        tfeat[k] = jnp.concatenate(rows, 0).T[:, :48].astype(BF16)
        return 0

    def source_block(pos_ref, nrm_ref, scl_ref, dsp_ref, first, factor, k, _):
        lane = pl.ds(pl.multiple_of(k * BLK, BLK), BLK)
        p = pos_ref[:, lane] - centre
        q1, q2, q3 = split(quads(p, jnp.sum(p * p, axis=0, keepdims=True) + 0.25), 3)
        s = scl_ref[pl.ds(k, 1), :]
        if factor is not None:
            s = jnp.where(factor, s, 0.0)
        r1, r2, r3 = split(quads(nrm_ref[:, lane] * s, s), 3)
        ahead = [
            jnp.where(is3, 1.0, jnp.where(is7 | low4, q1, q2)),
            jnp.where(is3, 1.0, jnp.where(low4, q1, q2)),
            jnp.where(is3, 1.0, jnp.where(low4, q1, q3)),
            zeros8,
            zeros8,
            zeros8,
        ]
        align = [
            zeros8,
            zeros8,
            zeros8,
            jnp.where(low4, r1, r2),
            jnp.where(low4, r1, r2),
            jnp.where(low4, r1, r3),
        ]
        sfeat[first + k, :, :BLK] = jnp.concatenate(ahead, 0).astype(BF16)
        sfeat[first + k, :, BLK:] = jnp.concatenate(align, 0).astype(BF16)
        d = dsp_ref[:, lane]
        d1, d2 = split(quads(d, jnp.zeros((1, BLK), F32)), 2)
        both = jnp.concatenate([jnp.where(low4, d1, d2), zeros8], 0).astype(BF16)
        dfeat[first + k, :, :BLK] = both
        dfeat[first + k, :, BLK:] = both
        return 0

    lax.fori_loop(0, NB, target_block, 0)
    lax.fori_loop(0, NB, functools.partial(source_block, pos, nrm, scl, dsp, NB, None), 0)

    slot = lax.broadcasted_iota(jnp.int32, (2 * NB, PMAX), 1)
    block = lax.broadcasted_iota(jnp.int32, (2 * NB, PMAX), 0)
    tgt = pair_rows[0:1, :] + NB
    src = pair_rows[1:2, :]
    live = slot < count[0]
    onehot[0] = jnp.where(live & (block == tgt), 1.0, 0.0).astype(BF16)
    onehot[1] = jnp.where(live & (block == src) & (src != tgt), 1.0, 0.0).astype(BF16)

    element = (
        lax.broadcasted_iota(jnp.int32, (NB, BLK), 0) * BLK
        + lax.broadcasted_iota(jnp.int32, (NB, BLK), 1)
    )
    partner = element + off[...]
    part_row = partner >> 7
    part_lane = partner & 127
    inside = jnp.where((me < devices - 1) | (partner < NB * BLK), 0.5, 0.0).astype(F32)
    iota_lane = lax.broadcasted_iota(jnp.int32, (BLK, BLK), 0)
    iota_row = lax.broadcasted_iota(jnp.int32, (2 * NB, BLK), 0)
    for k in range(NB):
        lane = pl.ds(k * BLK, BLK)
        lanes_hot[:, lane] = jnp.where(iota_lane == part_lane[k : k + 1], 1.0, 0.0).astype(BF16)
        rows_hot[:, lane] = jnp.where(iota_row == part_row[k : k + 1], 1.0, 0.0).astype(BF16)

    def gather(ref):
        out = []
        for v in range(NB // 8):
            lane = part_lane[8 * v : 8 * v + 8]
            hot = part_row[8 * v : 8 * v + 8]
            acc = jnp.zeros((8, BLK), F32)
            for h in range(8 * v, 8 * v + 8 + NB):
                line = jnp.broadcast_to(ref[h : h + 1, :], (8, BLK))
                got = jnp.take_along_axis(line, lane, axis=1, mode="promise_in_bounds")
                acc = jnp.where(hot == h, got, acc)
            out.append(acc)
        return jnp.concatenate(out, 0)

    def scatter(flux):
        top = flux.astype(BF16)
        rest = (flux - top.astype(F32)).astype(BF16)
        for k in range(NB):
            lane = pl.ds(k * BLK, BLK)
            hot = rows_hot[:, lane]
            spread[: 2 * NB, lane] = hot * top[k : k + 1]
            spread[2 * NB :, lane] = hot * rest[k : k + 1]
        both = lax.dot_general(spread[...], lanes_hot[...], NT, preferred_element_type=F32)
        return both[: 2 * NB] + both[2 * NB :]

    vec = inj[...]
    table_inj[:NB, :] = vec
    for copy in early:
        copy.wait_recv()
    vec_diff = vec - gather(table_inj)

    def apply(p, u):
        t = pairs[0, p] + NB
        s = pairs[1, p]
        hl = held[u]
        con_t[p] = lax.dot_general(dfeat[s], hl, NT, preferred_element_type=F32)[:8]
        back = jnp.dot(dfeat[t, :, :BLK], hl, preferred_element_type=F32)[:8]
        con_s[p] = back[:, :BLK] + back[:, BLK:]

    def evaluate(p, u):
        m = jnp.dot(tfeat[pairs[0, p]], sfeat[pairs[1, p]], preferred_element_type=F32)
        g = m[:, BLK:] * lax.rsqrt(m[:, :BLK])
        top = g.astype(BF16)
        held[u, :, :BLK] = top
        held[u, :, BLK:] = (g - top.astype(F32)).astype(BF16)

    def steps(i, _):
        for u in range(UNROLL):
            apply((i - 1) * UNROLL + u, u)
            evaluate(i * UNROLL + u, u)
        return 0

    for u in range(UNROLL):
        evaluate(u, u)
    lax.fori_loop(1, NB // UNROLL, steps, 0)
    for copy in frame:
        copy.wait_recv()
    lax.fori_loop(
        0, NB, functools.partial(source_block, prev_pos, prev_nrm, prev_scl, prev_dsp, 0, me > 0), 0
    )
    lax.fori_loop(NB // UNROLL, PMAX // UNROLL, steps, 0)
    for u in range(UNROLL):
        apply(PMAX - UNROLL + u, u)

    def component(c):
        def lines(ref):
            x = ref[:, c, :] + ref[:, c + 4, :]
            top = x.astype(BF16)
            return top, (x - top.astype(F32)).astype(BF16)

        out = jnp.zeros((2 * NB, BLK), F32)
        for which, ref in ((0, con_t), (1, con_s)):
            hot = onehot[which]
            for x in lines(ref):
                out = out + jnp.dot(hot, x, preferred_element_type=F32)
        return out

    first = component(0)
    near0[...] = first
    move0 = [send(near0, got0, 6, before), send(near0.at[pl.ds(0, NB)], got0_far, 7, before2)]
    second, third = component(1), component(2)
    near12[0] = second[:NB]
    near12[1] = third[:NB]
    move12 = send(near12, got12, 8, before)

    def cubed(scale, t):
        aperture = scale * (1.0 + 0.5 * jnp.tanh(t))
        return aperture * aperture * aperture

    for copy in move0:
        copy.wait_recv()
    traction0 = first[NB:] + got0[:NB, :]
    cube = cubed(base[...], traction0)
    table[:NB, :] = cube
    table[NB:, :] = cubed(base_next[...], got0[NB:, :] + got0_far[...])
    weight = inside * (cube + gather(table))

    flux = weight * vec_diff
    landed = scatter(flux)
    part = sto[...] * vec + flux - landed[:NB]
    landed_out[...] = landed[NB:]
    part_out[...] = part
    move_q = [send(landed_out, landed_in, 9, after), send(part_out, part_in, 10, before)]
    for copy in move_q:
        copy.wait_recv()
    q = part - landed_in[...]
    table[:NB, :] = q
    table[NB:, :] = part_in[...] - landed[NB:]
    q_diff = q - gather(table)
    flux = weight * q_diff

    def line(x):
        return jnp.sum(x, axis=0, keepdims=True)

    rows = [line(vec * vec), line(vec * q), line(q * q), line(sto[...] * q * q + flux * q_diff)]
    sums = jnp.concatenate(rows + [jnp.zeros((4, BLK), F32)], 0)

    def exchange(stage, sums, size, mate, got):
        if size == 1:
            return sums
        sums_out[stage] = sums
        for j in range(1, size):
            pltpu.make_async_remote_copy(
                src_ref=sums_out.at[stage],
                dst_ref=got.at[j - 1],
                send_sem=red_send.at[stage],
                recv_sem=red_recv.at[stage],
                device_id=mate(j),
                device_id_type=MESH,
            ).start()

    def collect(stage, sums, size, got):
        if size == 1:
            return sums
        pltpu.make_async_copy(got, got, red_recv.at[stage]).wait()
        for j in range(size - 1):
            sums = sums + got[j]
        return sums

    exchange(0, sums, grp_size, grp_mate, sums_grp)
    landed = scatter(flux)
    landed2_out[...] = landed[NB:]
    move_u = send(landed2_out, landed2_in, 11, after)
    u_part = sto[...] * q + flux - landed[:NB]
    sums = collect(0, sums, grp_size, sums_grp)
    exchange(1, sums, low_size, low_mate, sums_low)
    move12.wait_recv()
    full = [traction0, second[NB:] + got12[0], third[NB:] + got12[1]]
    for k in range(NB):
        rows = [x[k : k + 1] for x in full]
        traction[:, pl.ds(k * BLK, BLK)] = jnp.concatenate(rows, 0)
    sums = collect(1, sums, low_size, sums_low)
    exchange(2, sums, high_size, high_mate, sums_high)
    move_u.wait_recv()
    u = u_part - landed2_in[...]
    sums = collect(2, sums, high_size, sums_high)

    total = jnp.sum(sums, axis=1, keepdims=True)
    rr0, r0q, qq, qu = (total[j : j + 1] for j in range(4))
    alpha0 = rr0 / r0q
    rr1 = alpha0 * alpha0 * qq - rr0
    beta = rr1 / rr0
    alpha1 = rr1 / (r0q - 2.0 * alpha0 * qq + alpha0 * alpha0 * qu - beta * rr1 / alpha0)
    keep = 1.0 + beta
    r1 = vec - alpha0 * q
    residual[...] = r1 - alpha1 * (keep * q - alpha0 * u)
    pressure[...] = alpha0 * vec + alpha1 * (r1 + beta * vec)

    for copy in frame + early + move0 + [move12] + move_q + [move_u]:
        copy.wait_send()
    for stage, (size, got) in enumerate(
        ((grp_size, sums_grp), (low_size, sums_low), (high_size, sums_high))
    ):
        if size > 1:
            pltpu.make_async_copy(got, got, red_send.at[stage]).wait()


def shards(
    grp_size,
    seg_size,
    positions,
    normals,
    scales,
    displacement,
    pair_list,
    pair_count,
    base_aperture,
    storage,
    injection,
    link_offset,
):
    low_size = 8 if seg_size % 8 == 0 else 2
    high_size = seg_size // low_size
    square = (NB, BLK)
    vmem = pl.BlockSpec(memory_space=pltpu.VMEM)
    smem = pl.BlockSpec(memory_space=pltpu.SMEM)
    scratch = [
        pltpu.VMEM((3, NB * BLK), F32),
        pltpu.VMEM((3, NB * BLK), F32),
        pltpu.VMEM(square, F32),
        pltpu.VMEM((3, NB * BLK), F32),
        pltpu.VMEM(square, F32),
        pltpu.VMEM((2 * NB, BLK), F32),
        pltpu.VMEM((NB, BLK, 48), BF16),
        pltpu.VMEM((2 * NB, 48, 2 * BLK), BF16),
        pltpu.VMEM((2 * NB, 16, 2 * BLK), BF16),
        pltpu.VMEM((UNROLL, BLK, 2 * BLK), BF16),
        pltpu.VMEM((PMAX, 8, BLK), F32),
        pltpu.VMEM((PMAX, 8, BLK), F32),
        pltpu.VMEM((2 * NB, BLK), F32),
        pltpu.VMEM((2, NB, BLK), F32),
        pltpu.VMEM((2 * NB, BLK), F32),
        pltpu.VMEM(square, F32),
        pltpu.VMEM((2, NB, BLK), F32),
        pltpu.VMEM((2, 2 * NB, PMAX), BF16),
        pltpu.VMEM((BLK, NB * BLK), BF16),
        pltpu.VMEM((2 * NB, NB * BLK), BF16),
        pltpu.VMEM((4 * NB, NB * BLK), BF16),
        pltpu.VMEM((2 * NB, BLK), F32),
        pltpu.VMEM(square, F32),
        pltpu.VMEM(square, F32),
        pltpu.VMEM(square, F32),
        pltpu.VMEM(square, F32),
        pltpu.VMEM(square, F32),
        pltpu.VMEM(square, F32),
        pltpu.VMEM((3, 8, BLK), F32),
        pltpu.VMEM((max(grp_size - 1, 1), 8, BLK), F32),
        pltpu.VMEM((max(low_size - 1, 1), 8, BLK), F32),
        pltpu.VMEM((max(high_size - 1, 1), 8, BLK), F32),
        pltpu.SemaphoreType.DMA((12,)),
        pltpu.SemaphoreType.DMA((12,)),
        pltpu.SemaphoreType.DMA((3,)),
        pltpu.SemaphoreType.DMA((3,)),
    ]
    traction, pressure, residual = pl.pallas_call(
        functools.partial(kernel, grp_size, seg_size, low_size),
        out_shape=(
            jax.ShapeDtypeStruct((3, NB * BLK), F32),
            jax.ShapeDtypeStruct(square, F32),
            jax.ShapeDtypeStruct(square, F32),
        ),
        in_specs=[smem, smem] + [vmem] * 9,
        out_specs=(vmem, vmem, vmem),
        scratch_shapes=scratch,
        compiler_params=pltpu.CompilerParams(
            collective_id=0, has_side_effects=True, vmem_limit_bytes=48 << 20
        ),
        name="network",
    )(
        pair_list,
        pair_count,
        positions,
        normals,
        scales.reshape(square),
        displacement,
        pair_list,
        base_aperture.reshape(square),
        storage.reshape(square),
        injection.reshape(square),
        link_offset.reshape(square),
    )
    return traction, pressure.reshape(-1), residual.reshape(-1)


def solution(mesh):
    return jax.shard_map(
        functools.partial(shards, mesh.shape["grp"], mesh.shape["seg"]),
        mesh=mesh,
        in_specs=(
            P(None, ("grp", "seg")),
            P(None, ("grp", "seg")),
            P(("grp", "seg")),
            P(None, ("grp", "seg")),
            P(None, ("grp", "seg")),
            P(("grp", "seg")),
            P(("grp", "seg")),
            P(("grp", "seg")),
            P(("grp", "seg")),
            P(("grp", "seg")),
        ),
        out_specs=(P(None, ("grp", "seg")), P(("grp", "seg")), P(("grp", "seg"))),
        check_vma=False,
    )
```

time: 630 us -> 62.7 us (0.10)
  blocking collectives: 321 us -> 0 us
  starting transfers between devices: 104 us -> 0 us
  local copies, waits for them, and re-layouts: 89.7 us -> 8.62 us
  other arithmetic: 56 us -> 0 us
  Pallas kernels: 0 us -> 51.9 us
  waiting for transfers between devices: 30.2 us -> 0 us
  matrix products: 22.1 us -> 0 us
    psum x3 -> x0, blocking collectives: 321 us -> none  [the longest x2 228 us: residual_squares(): return lax.psum(jnp.sum(vec * vec), ('grp', 'seg'))]
    ppermute x10 -> x0, starting transfers between devices: 104 us -> none  [from_behind(): return lax.ppermute(block, axis, route)]
    gather x33 -> x0, local copies, waits for them, and re-layouts: 87.2 us -> none  [the longest x2 46.1 us: flow_apply(): flux = weight * (vec - jnp.concatenate([vec, after])[target])]
    pallas_call x0 -> x1, Pallas kernels: none -> 51.9 us  [shards(): pl.pallas_call(functools.partial(kernel, grp_size, seg_size, low_size), o...]
    scatter-add x8 -> x0, other arithmetic: 50.5 us -> none  [the longest x2 43.9 us: flow_apply(): landed = jnp.zeros((2 * count,), jnp.float32).at[target].add(-flux)]
    ppermute x10 -> x0, waiting for transfers between devices: 30.2 us -> none  [from_behind(): return lax.ppermute(block, axis, route)]
    dot_general x6 -> x0, matrix products: 22.1 us -> none  [the longest x3 12.1 us: one(): jnp.einsum('gab,cgb->cga', kern, dsp[:, src], precision=lax.Precision.HIG...]
    unnamed x18 -> x21, local copies, waits for them, and re-layouts: 2.17 us -> 8.62 us
  transfers between devices with their start and end apart: 10 -> 0, of which waited for: 4 -> 0; matrix products, arithmetic and copies ran while one was open for 12% -> 0% of each run, Pallas kernels for 0% -> 0%
where the time goes in v1:
time: 62.7 us; the launch traced here: 61.8 us
  Pallas kernels  51.9 us (83%)
  local copies, waits for them, and re-layouts  8.62 us (14%)
  between operations  1.3 us (2%)
    pallas_call x1, Pallas kernels, shards(): pl.pallas_call(functools.partial(kernel, grp_size, seg_size, low_size), o...  51.9 us
    unnamed x21, local copies, waits for them, and re-layouts  8.62 us

profile of v1, /device:TPU:1, one launch (start us, length us, event | category | flops | bytes accessed | tf_op | source)
XLA Modules:
  0.0 61.8 jit_solution(11454616261922614838)
XLA Ops:
  1.3 0.0 copy-start.8
  1.3 0.7 %copy-done.8 = s32[2,160]{1,0:T(2,128)S(1)} copy-done((s32[2,160]{1,0:T(2,128)S(1)}, s32[2,160]{1,0:T(2,128)}, u32[]{:S(2)}) %copy-start.8) | copy-done | bytes 1304
  2.0 0.0 copy-start
  2.0 0.8 %copy-done = f32[3,4096]{1,0:T(4,128)S(1)} copy-done((f32[3,4096]{1,0:T(4,128)S(1)}, f32[3,4096]{1,0:T(4,128)}, u32[]{:S(2)}) %copy-start) | copy-done | bytes 49176
  2.8 0.0 copy-start.1
  2.8 0.8 %copy-done.1 = f32[3,4096]{1,0:T(4,128)S(1)} copy-done((f32[3,4096]{1,0:T(4,128)S(1)}, f32[3,4096]{1,0:T(4,128)}, u32[]{:S(2)}) %copy-start.1) | copy-done | bytes 49176
  3.6 0.0 copy-start.2
  3.6 0.8 %copy-done.2 = f32[3,4096]{1,0:T(4,128)S(1)} copy-done((f32[3,4096]{1,0:T(4,128)S(1)}, f32[3,4096]{1,0:T(4,128)}, u32[]{:S(2)}) %copy-start.2) | copy-done | bytes 49176
  4.5 0.0 copy-start.3
  4.5 0.7 %copy-done.3 = f32[4096]{0:T(1024)S(1)} copy-done((f32[4096]{0:T(1024)S(1)}, f32[4096]{0:T(1024)}, u32[]{:S(2)}) %copy-start.3) | copy-done | bytes 16408
  5.2 0.0 copy-start.4
  5.2 0.7 %copy-done.4 = f32[4096]{0:T(1024)S(1)} copy-done((f32[4096]{0:T(1024)S(1)}, f32[4096]{0:T(1024)}, u32[]{:S(2)}) %copy-start.4) | copy-done | bytes 16408
  5.9 0.0 copy-start.5
  5.9 0.7 %copy-done.5 = f32[4096]{0:T(1024)S(1)} copy-done((f32[4096]{0:T(1024)S(1)}, f32[4096]{0:T(1024)}, u32[]{:S(2)}) %copy-start.5) | copy-done | bytes 16408
  6.6 0.0 copy-start.6
  6.6 0.7 %copy-done.6 = f32[4096]{0:T(1024)S(1)} copy-done((f32[4096]{0:T(1024)S(1)}, f32[4096]{0:T(1024)}, u32[]{:S(2)}) %copy-start.6) | copy-done | bytes 16408
  7.4 0.0 copy-start.7
  7.4 0.7 %copy-done.7 = s32[4096]{0:T(1024)S(1)} copy-done((s32[4096]{0:T(1024)S(1)}, s32[4096]{0:T(1024)}, u32[]{:S(2)}) %copy-start.7) | copy-done | bytes 16408
  8.1 51.9 %network.1 = (f32[3,4096]{1,0:T(4,128)S(1)}, f32[32,128]{1,0:T(8,128)S(1)}, f32[32,128]{1,0:T(8,128)S(1)}) custom-call(s32[2,160]{1,0:T(2,128)S(1)} %copy-done.8, s32[1]{0:T(128)S(6)} %copy.16.count, f32[3,4096]{1,0:T(4,128)S(1)} %copy-done, f32[3,4096]{1,0:T(4,128)S(1)} %copy-done.1, f32[32,128]{1,0:T(8,128)S(1)} %bitcast.7, f32[3,4096]{1,0:T(4,128)S(1)} %copy-done.2, ...), custom_call_target="tpu_custom_call" | custom-call | tf_op jit(solution)/shard_map/network/pallas_call | solution.py:460
  59.9 0.6 %copy.17 = f32[3,4096]{1,0:T(4,128)} copy(f32[3,4096]{1,0:T(4,128)S(1)} %get-tuple-element.12) | data formatting | bytes 98304
  60.6 0.6 copy.18
  61.2 0.6 copy.19
Async XLA Ops:
  1.3 0.7 %copy-start.8 = (s32[2,160]{1,0:T(2,128)S(1)}, s32[2,160]{1,0:T(2,128)}, u32[]{:S(2)}) copy-start(s32[2,160]{1,0:T(2,128)} %pair_rows.1) | copy-start | bytes 3844
  2.0 0.8 %copy-start = (f32[3,4096]{1,0:T(4,128)S(1)}, f32[3,4096]{1,0:T(4,128)}, u32[]{:S(2)}) copy-start(f32[3,4096]{1,0:T(4,128)} %pos.1) | copy-start | bytes 147460
  2.8 0.8 %copy-start.1 = (f32[3,4096]{1,0:T(4,128)S(1)}, f32[3,4096]{1,0:T(4,128)}, u32[]{:S(2)}) copy-start(f32[3,4096]{1,0:T(4,128)} %nrm.1) | copy-start | bytes 147460
  3.6 0.8 %copy-start.2 = (f32[3,4096]{1,0:T(4,128)S(1)}, f32[3,4096]{1,0:T(4,128)}, u32[]{:S(2)}) copy-start(f32[3,4096]{1,0:T(4,128)} %dsp.1) | copy-start | bytes 147460
  4.5 0.7 %copy-start.3 = (f32[4096]{0:T(1024)S(1)}, f32[4096]{0:T(1024)}, u32[]{:S(2)}) copy-start(f32[4096]{0:T(1024)} %param.12) | copy-start | bytes 49156
  5.2 0.7 %copy-start.4 = (f32[4096]{0:T(1024)S(1)}, f32[4096]{0:T(1024)}, u32[]{:S(2)}) copy-start(f32[4096]{0:T(1024)} %param.16) | copy-start | bytes 49156
  5.9 0.7 %copy-start.5 = (f32[4096]{0:T(1024)S(1)}, f32[4096]{0:T(1024)}, u32[]{:S(2)}) copy-start(f32[4096]{0:T(1024)} %param.17) | copy-start | bytes 49156
  6.6 0.7 %copy-start.6 = (f32[4096]{0:T(1024)S(1)}, f32[4096]{0:T(1024)}, u32[]{:S(2)}) copy-start(f32[4096]{0:T(1024)} %param.18) | copy-start | bytes 49156
  7.4 0.7 %copy-start.7 = (s32[4096]{0:T(1024)S(1)}, s32[4096]{0:T(1024)}, u32[]{:S(2)}) copy-start(s32[4096]{0:T(1024)} %param.19) | copy-start | bytes 49156

commit v2 on v1

--- a/solution.py
+++ b/solution.py
@@ -14,7 +14,7 @@
 BF16 = jnp.bfloat16
 MESH = pl.DeviceIdType.MESH
 NT = (((1,), (1,)), ((), ()))
-UNROLL = 8
+UNROLL = 16
 
 
 def split(x, parts):
@@ -31,23 +31,30 @@
 
 
 def kernel(
-    grp_size,
-    seg_size,
-    low_size,
-    pairs,
-    count,
+    sizes,
+    pos_in,
+    nrm_in,
+    scl_in,
+    dsp_in,
+    pair_in,
+    count_in,
+    base_in,
+    sto_in,
+    inj_in,
+    off_in,
+    traction,
+    pressure,
+    residual,
     pos,
     nrm,
     scl,
     dsp,
+    pairs,
     pair_rows,
+    count,
     base,
     sto,
-    inj,
     off,
-    traction,
-    pressure,
-    residual,
     prev_pos,
     prev_nrm,
     prev_scl,
@@ -57,6 +64,7 @@
     tfeat,
     sfeat,
     dfeat,
+    columns,
     held,
     con_t,
     con_s,
@@ -77,16 +85,17 @@
     landed2_out,
     landed2_in,
     sums_out,
-    sums_grp,
-    sums_low,
-    sums_high,
+    sums_near,
+    sums_far,
     send_sem,
     recv_sem,
     red_send,
     red_recv,
+    load_sem,
 ):
+    x_size, core_size, high_size, low_size = sizes
+    grp_size, seg_size = x_size * core_size, high_size * low_size
     devices = grp_size * seg_size
-    high_size = seg_size // low_size
     grp = lax.axis_index("grp")
     seg = lax.axis_index("seg")
     me = grp * seg_size + seg
@@ -95,22 +104,44 @@
         to = lax.rem(me + shift + devices, devices)
         return (to // seg_size, lax.rem(to, seg_size))
 
-    def grp_mate(j):
-        return (lax.rem(grp + j, grp_size), seg)
-
-    def low_mate(j):
-        return (grp, seg // low_size * low_size + lax.rem(lax.rem(seg, low_size) + j, low_size))
-
-    def high_mate(j):
-        return (grp, lax.rem(seg + j * low_size, seg_size))
-
+    def ring(index, size, low, shift):
+        digit = index // low
+        if size * low > 1:
+            digit = lax.rem(digit, size)
+        return index + (lax.rem(digit + shift, size) - digit) * low
+
+    def mate(stage, j):
+        if stage == 0:
+            return (ring(grp, core_size, 1, j % core_size), ring(seg, low_size, 1, j // core_size))
+        return (
+            ring(grp, x_size, core_size, j % x_size),
+            ring(seg, high_size, low_size, j // x_size),
+        )
+
+    groups = (core_size * low_size, x_size * high_size)
     mates = [device(shift) for shift in (1, -1, 2, -2)]
-    mates += [grp_mate(j) for j in range(1, grp_size)]
-    mates += [low_mate(j) for j in range(1, low_size)]
-    mates += [high_mate(j) for j in range(1, high_size)]
+    mates += [mate(stage, j) for stage in (0, 1) for j in range(1, groups[stage])]
     barrier = pltpu.get_barrier_semaphore()
-    for mate in mates:
-        pl.semaphore_signal(barrier, inc=1, device_id=mate, device_id_type=MESH)
+    for to in mates:
+        pl.semaphore_signal(barrier, inc=1, device_id=to, device_id_type=MESH)
+    loads = {}
+    for slot, (src, dst) in enumerate(
+        (
+            (pos_in, pos),
+            (nrm_in, nrm),
+            (scl_in, scl),
+            (dsp_in, dsp),
+            (pair_in, pairs),
+            (pair_in, pair_rows),
+            (count_in, count),
+            (inj_in, table_inj.at[pl.ds(0, NB)]),
+            (off_in, off),
+            (base_in, base),
+            (sto_in, sto),
+        )
+    ):
+        loads[slot] = pltpu.make_async_copy(src, dst, load_sem.at[slot])
+        loads[slot].start()
     pl.semaphore_wait(barrier, len(mates))
 
     def send(src, dst, slot, to):
@@ -127,15 +158,18 @@
 
     after, before, before2 = device(1), device(-1), device(-2)
     frame = [
-        send(pos, prev_pos, 0, after),
-        send(nrm, prev_nrm, 1, after),
-        send(scl, prev_scl, 2, after),
-        send(dsp, prev_dsp, 3, after),
+        send(pos_in, prev_pos, 0, after),
+        send(nrm_in, prev_nrm, 1, after),
+        send(scl_in, prev_scl, 2, after),
+        send(dsp_in, prev_dsp, 3, after),
     ]
     early = [
-        send(base, base_next, 4, before),
-        send(inj, table_inj.at[pl.ds(NB, NB)], 5, before),
+        send(base_in, base_next, 4, before),
+        send(inj_in, table_inj.at[pl.ds(NB, NB)], 5, before),
     ]
+
+    for load in loads.values():
+        load.wait()
 
     row = lax.broadcasted_iota(jnp.int32, (8, BLK), 0)
     low4 = row < 4
@@ -161,8 +195,13 @@
             r2,
             jnp.where(low4, r3, r1),
         ]
-        rows += [zeros8] * 10
-        tfeat[k] = jnp.concatenate(rows, 0).T[:, :48].astype(BF16)
+        d = dsp[:, lane]
+        rows += [jnp.concatenate([d, jnp.zeros((5, BLK), F32)], 0)]
+        rows += [zeros8] * 9
+        upright = jnp.concatenate(rows, 0).T
+        tfeat[k] = upright[:, :48].astype(BF16)
+        for c in range(3):
+            columns[k, c] = jnp.broadcast_to(upright[:, 48 + c : 49 + c], (BLK, BLK))
         return 0
 
     def source_block(pos_ref, nrm_ref, scl_ref, dsp_ref, first, factor, k, _):
@@ -217,11 +256,12 @@
     part_row = partner >> 7
     part_lane = partner & 127
     inside = jnp.where((me < devices - 1) | (partner < NB * BLK), 0.5, 0.0).astype(F32)
-    iota_lane = lax.broadcasted_iota(jnp.int32, (BLK, BLK), 0)
+    iota_lane = lax.broadcasted_iota(jnp.int32, (BLK, BLK), 1).astype(F32)
     iota_row = lax.broadcasted_iota(jnp.int32, (2 * NB, BLK), 0)
+    upright_lane = part_lane.astype(F32).T
     for k in range(NB):
         lane = pl.ds(k * BLK, BLK)
-        lanes_hot[:, lane] = jnp.where(iota_lane == part_lane[k : k + 1], 1.0, 0.0).astype(BF16)
+        lanes_hot[lane, :] = jnp.where(iota_lane == upright_lane[:, k : k + 1], 1.0, 0.0).astype(BF16)
         rows_hot[:, lane] = jnp.where(iota_row == part_row[k : k + 1], 1.0, 0.0).astype(BF16)
 
     def gather(ref):
@@ -238,45 +278,49 @@
         return jnp.concatenate(out, 0)
 
     def scatter(flux):
-        top = flux.astype(BF16)
-        rest = (flux - top.astype(F32)).astype(BF16)
+        top, rest = split(flux, 2)
         for k in range(NB):
             lane = pl.ds(k * BLK, BLK)
             hot = rows_hot[:, lane]
-            spread[: 2 * NB, lane] = hot * top[k : k + 1]
-            spread[2 * NB :, lane] = hot * rest[k : k + 1]
-        both = lax.dot_general(spread[...], lanes_hot[...], NT, preferred_element_type=F32)
+            for first, x in ((0, top), (2 * NB, rest)):
+                line = jnp.broadcast_to(x[k : k + 1], (16, BLK)).astype(BF16)
+                spread[first : first + 2 * NB, lane] = hot * jnp.concatenate([line] * 4, 0)
+        both = jnp.dot(spread[...], lanes_hot[...], preferred_element_type=F32)
         return both[: 2 * NB] + both[2 * NB :]
 
-    vec = inj[...]
-    table_inj[:NB, :] = vec
+    vec = table_inj[:NB, :]
     for copy in early:
         copy.wait_recv()
     vec_diff = vec - gather(table_inj)
 
-    def apply(p, u):
-        t = pairs[0, p] + NB
-        s = pairs[1, p]
-        hl = held[u]
-        con_t[p] = lax.dot_general(dfeat[s], hl, NT, preferred_element_type=F32)[:8]
-        back = jnp.dot(dfeat[t, :, :BLK], hl, preferred_element_type=F32)[:8]
-        con_s[p] = back[:, :BLK] + back[:, BLK:]
-
-    def evaluate(p, u):
-        m = jnp.dot(tfeat[pairs[0, p]], sfeat[pairs[1, p]], preferred_element_type=F32)
+    def apply(i, u):
+        s = pairs[1, i * UNROLL + u]
+        out = lax.dot_general(dfeat[s], held[u], NT, preferred_element_type=F32)
+        out = out[:4] + out[4:8]
+        for c in range(3):
+            con_t[c, i * (UNROLL // 8) + u // 8, u % 8 : u % 8 + 1, :] = out[c : c + 1]
+
+    def evaluate(i, u):
+        p = i * UNROLL + u
+        t = pairs[0, p]
+        m = jnp.dot(tfeat[t], sfeat[pairs[1, p]], preferred_element_type=F32)
         g = m[:, BLK:] * lax.rsqrt(m[:, :BLK])
         top = g.astype(BF16)
         held[u, :, :BLK] = top
         held[u, :, BLK:] = (g - top.astype(F32)).astype(BF16)
+        for c in range(3):
+            con_s[c, i * (UNROLL // 8) + u // 8, u % 8 : u % 8 + 1, :] = jnp.sum(
+                g * columns[t, c], axis=0, keepdims=True
+            )
 
     def steps(i, _):
         for u in range(UNROLL):
-            apply((i - 1) * UNROLL + u, u)
-            evaluate(i * UNROLL + u, u)
+            apply(i - 1, u)
+            evaluate(i, u)
         return 0
 
     for u in range(UNROLL):
-        evaluate(u, u)
+        evaluate(0, u)
     lax.fori_loop(1, NB // UNROLL, steps, 0)
     for copy in frame:
         copy.wait_recv()
@@ -285,27 +329,22 @@
     )
     lax.fori_loop(NB // UNROLL, PMAX // UNROLL, steps, 0)
     for u in range(UNROLL):
-        apply(PMAX - UNROLL + u, u)
-
-    def component(c):
-        def lines(ref):
-            x = ref[:, c, :] + ref[:, c + 4, :]
-            top = x.astype(BF16)
-            return top, (x - top.astype(F32)).astype(BF16)
-
-        out = jnp.zeros((2 * NB, BLK), F32)
+        apply(PMAX // UNROLL - 1, u)
+
+    def blocks(parts):
+        out = jnp.zeros((2 * NB, BLK * len(parts)), F32)
         for which, ref in ((0, con_t), (1, con_s)):
-            hot = onehot[which]
-            for x in lines(ref):
-                out = out + jnp.dot(hot, x, preferred_element_type=F32)
+            x = jnp.concatenate([ref[c].reshape(PMAX, BLK) for c in parts], 1)
+            for y in split(x, 2):
+                out = out + jnp.dot(onehot[which], y.astype(BF16), preferred_element_type=F32)
         return out
 
-    first = component(0)
+    first = blocks((0,))
     near0[...] = first
     move0 = [send(near0, got0, 6, before), send(near0.at[pl.ds(0, NB)], got0_far, 7, before2)]
-    second, third = component(1), component(2)
-    near12[0] = second[:NB]
-    near12[1] = third[:NB]
+    others = blocks((1, 2))
+    near12[0] = others[:NB, :BLK]
+    near12[1] = others[:NB, BLK:]
     move12 = send(near12, got12, 8, before)
 
     def cubed(scale, t):
@@ -340,45 +379,53 @@
     rows = [line(vec * vec), line(vec * q), line(q * q), line(sto[...] * q * q + flux * q_diff)]
     sums = jnp.concatenate(rows + [jnp.zeros((4, BLK), F32)], 0)
 
-    def exchange(stage, sums, size, mate, got):
-        if size == 1:
-            return sums
+    def distance(stage, j):
+        if stage == 0:
+            wide, narrow, far = low_size, core_size, j // core_size
+        else:
+            wide, narrow, far = high_size, x_size, j // x_size
+        near = j % narrow
+        return min(far, wide - far) + min(near, narrow - near)
+
+    def exchange(stage, sums, got):
         sums_out[stage] = sums
-        for j in range(1, size):
+        order = sorted(range(1, groups[stage]), key=functools.partial(distance, stage))
+        for j in order[::-1]:
             pltpu.make_async_remote_copy(
                 src_ref=sums_out.at[stage],
                 dst_ref=got.at[j - 1],
                 send_sem=red_send.at[stage],
                 recv_sem=red_recv.at[stage],
-                device_id=mate(j),
+                device_id=mate(stage, j),
                 device_id_type=MESH,
             ).start()
 
-    def collect(stage, sums, size, got):
-        if size == 1:
-            return sums
+    def collect(stage, sums, got):
         pltpu.make_async_copy(got, got, red_recv.at[stage]).wait()
-        for j in range(size - 1):
-            sums = sums + got[j]
-        return sums
-
-    exchange(0, sums, grp_size, grp_mate, sums_grp)
+        parts = [sums] + [got[j] for j in range(groups[stage] - 1)]
+        while len(parts) > 1:
+            parts = [sum(parts[j : j + 2]) for j in range(0, len(parts), 2)]
+        return parts[0]
+
+    exchange(0, sums, sums_near)
     landed = scatter(flux)
     landed2_out[...] = landed[NB:]
     move_u = send(landed2_out, landed2_in, 11, after)
     u_part = sto[...] * q + flux - landed[:NB]
-    sums = collect(0, sums, grp_size, sums_grp)
-    exchange(1, sums, low_size, low_mate, sums_low)
+    sums = collect(0, sums, sums_near)
+    exchange(1, sums, sums_far)
     move12.wait_recv()
-    full = [traction0, second[NB:] + got12[0], third[NB:] + got12[1]]
+    full = [
+        traction0,
+        others[NB:, :BLK] + got12[0],
+        others[NB:, BLK:] + got12[1],
+    ]
     for k in range(NB):
         rows = [x[k : k + 1] for x in full]
         traction[:, pl.ds(k * BLK, BLK)] = jnp.concatenate(rows, 0)
-    sums = collect(1, sums, low_size, sums_low)
-    exchange(2, sums, high_size, high_mate, sums_high)
     move_u.wait_recv()
     u = u_part - landed2_in[...]
-    sums = collect(2, sums, high_size, sums_high)
+    sums = collect(1, sums, sums_far)
 
     total = jnp.sum(sums, axis=1, keepdims=True)
     rr0, r0q, qq, qu = (total[j : j + 1] for j in range(4))
@@ -393,11 +440,17 @@
 
     for copy in frame + early + move0 + [move12] + move_q + [move_u]:
         copy.wait_send()
-    for stage, (size, got) in enumerate(
-        ((grp_size, sums_grp), (low_size, sums_low), (high_size, sums_high))
-    ):
-        if size > 1:
-            pltpu.make_async_copy(got, got, red_send.at[stage]).wait()
+    pltpu.make_async_copy(sums_near, sums_near, red_send.at[0]).wait()
+    pltpu.make_async_copy(sums_far, sums_far, red_send.at[1]).wait()
+
+
+def deliver(traction_in, pressure_in, residual_in, traction, pressure, residual, sem):
+    refs = ((traction_in, traction), (pressure_in, pressure), (residual_in, residual))
+    copies = [pltpu.make_async_copy(a, b, sem.at[j]) for j, (a, b) in enumerate(refs)]
+    for copy in copies:
+        copy.start()
+    for copy in copies:
+        copy.wait()
 
 
 def shards(
@@ -416,10 +469,21 @@
 ):
     low_size = 8 if seg_size % 8 == 0 else 2
     high_size = seg_size // low_size
+    sizes = (grp_size // 2, 2, high_size, low_size)
     square = (NB, BLK)
     vmem = pl.BlockSpec(memory_space=pltpu.VMEM)
-    smem = pl.BlockSpec(memory_space=pltpu.SMEM)
+    anywhere = pl.BlockSpec(memory_space=pl.ANY)
     scratch = [
+        pltpu.VMEM((3, NB * BLK), F32),
+        pltpu.VMEM((3, NB * BLK), F32),
+        pltpu.VMEM(square, F32),
+        pltpu.VMEM((3, NB * BLK), F32),
+        pltpu.SMEM((2, PMAX), jnp.int32),
+        pltpu.VMEM((2, PMAX), jnp.int32),
+        pltpu.SMEM((1,), jnp.int32),
+        pltpu.VMEM(square, F32),
+        pltpu.VMEM(square, F32),
+        pltpu.VMEM(square, jnp.int32),
         pltpu.VMEM((3, NB * BLK), F32),
         pltpu.VMEM((3, NB * BLK), F32),
         pltpu.VMEM(square, F32),
@@ -429,16 +493,17 @@
         pltpu.VMEM((NB, BLK, 48), BF16),
         pltpu.VMEM((2 * NB, 48, 2 * BLK), BF16),
         pltpu.VMEM((2 * NB, 16, 2 * BLK), BF16),
+        pltpu.VMEM((NB, 3, BLK, BLK), F32),
         pltpu.VMEM((UNROLL, BLK, 2 * BLK), BF16),
-        pltpu.VMEM((PMAX, 8, BLK), F32),
-        pltpu.VMEM((PMAX, 8, BLK), F32),
+        pltpu.VMEM((3, PMAX // 8, 8, BLK), F32),
+        pltpu.VMEM((3, PMAX // 8, 8, BLK), F32),
         pltpu.VMEM((2 * NB, BLK), F32),
         pltpu.VMEM((2, NB, BLK), F32),
         pltpu.VMEM((2 * NB, BLK), F32),
         pltpu.VMEM(square, F32),
         pltpu.VMEM((2, NB, BLK), F32),
         pltpu.VMEM((2, 2 * NB, PMAX), BF16),
-        pltpu.VMEM((BLK, NB * BLK), BF16),
+        pltpu.VMEM((NB * BLK, BLK), BF16),
         pltpu.VMEM((2 * NB, NB * BLK), BF16),
         pltpu.VMEM((4 * NB, NB * BLK), BF16),
         pltpu.VMEM((2 * NB, BLK), F32),
@@ -448,42 +513,50 @@
         pltpu.VMEM(square, F32),
         pltpu.VMEM(square, F32),
         pltpu.VMEM(square, F32),
-        pltpu.VMEM((3, 8, BLK), F32),
-        pltpu.VMEM((max(grp_size - 1, 1), 8, BLK), F32),
-        pltpu.VMEM((max(low_size - 1, 1), 8, BLK), F32),
-        pltpu.VMEM((max(high_size - 1, 1), 8, BLK), F32),
+        pltpu.VMEM((2, 8, BLK), F32),
+        pltpu.VMEM((2 * low_size - 1, 8, BLK), F32),
+        pltpu.VMEM((grp_size // 2 * high_size - 1, 8, BLK), F32),
         pltpu.SemaphoreType.DMA((12,)),
         pltpu.SemaphoreType.DMA((12,)),
-        pltpu.SemaphoreType.DMA((3,)),
-        pltpu.SemaphoreType.DMA((3,)),
+        pltpu.SemaphoreType.DMA((2,)),
+        pltpu.SemaphoreType.DMA((2,)),
+        pltpu.SemaphoreType.DMA((11,)),
     ]
-    traction, pressure, residual = pl.pallas_call(
-        functools.partial(kernel, grp_size, seg_size, low_size),
-        out_shape=(
-            jax.ShapeDtypeStruct((3, NB * BLK), F32),
-            jax.ShapeDtypeStruct(square, F32),
-            jax.ShapeDtypeStruct(square, F32),
-        ),
-        in_specs=[smem, smem] + [vmem] * 9,
+    shapes = (
+        jax.ShapeDtypeStruct((3, NB * BLK), F32),
+        jax.ShapeDtypeStruct(square, F32),
+        jax.ShapeDtypeStruct(square, F32),
+    )
+    outs = pl.pallas_call(
+        functools.partial(kernel, sizes),
+        out_shape=shapes,
+        in_specs=[anywhere] * 10,
         out_specs=(vmem, vmem, vmem),
         scratch_shapes=scratch,
         compiler_params=pltpu.CompilerParams(
-            collective_id=0, has_side_effects=True, vmem_limit_bytes=48 << 20
+            collective_id=0, has_side_effects=True, vmem_limit_bytes=56 << 20
         ),
         name="network",
     )(
-        pair_list,
-        pair_count,
         positions,
         normals,
         scales.reshape(square),
         displacement,
         pair_list,
+        pair_count,
         base_aperture.reshape(square),
         storage.reshape(square),
         injection.reshape(square),
         link_offset.reshape(square),
     )
+    traction, pressure, residual = pl.pallas_call(
+        deliver,
+        out_shape=shapes,
+        in_specs=[vmem] * 3,
+        out_specs=(anywhere,) * 3,
+        scratch_shapes=[pltpu.SemaphoreType.DMA((3,))],
+        name="deliver",
+    )(*outs)
     return traction, pressure.reshape(-1), residual.reshape(-1)
 
 

time: 62.7 us -> 57.7 us (0.920); the launches traced: 61.8 us -> 57.5 us
  local copies, waits for them, and re-layouts: 8.62 us -> 0 us
  Pallas kernels: 51.9 us -> 56.2 us
    unnamed x21 -> x0, local copies, waits for them, and re-layouts: 8.62 us -> none
    pallas_call x1 -> x2, Pallas kernels: 51.9 us -> 56.2 us  [the longest x1 54.7 us: shards(): pl.pallas_call(functools.partial(kernel, sizes), out_shape=shapes, in_spe...]
where the time goes in v2:
time: 57.7 us; the launch traced here: 57.5 us
  Pallas kernels  56.2 us (97%)
  between operations  1.29 us (2%)
    pallas_call x1, Pallas kernels, shards(): pl.pallas_call(functools.partial(kernel, sizes), out_shape=shapes, in_spe...  54.7 us
    pallas_call x1, Pallas kernels, shards(): pl.pallas_call(deliver, out_shape=shapes, in_specs=[vmem] * 3, out_specs=...  1.52 us

profile of v2, /device:TPU:1, one launch (start us, length us, event | category | flops | bytes accessed | tf_op | source)
XLA Modules:
  0.0 57.5 jit_solution(1503934965905427737)
XLA Ops:
  1.3 54.7 %network.1 = (f32[3,4096]{1,0:T(4,128)}, f32[32,128]{1,0:T(8,128)}, f32[32,128]{1,0:T(8,128)}) custom-call(f32[3,4096]{1,0:T(4,128)} %pos_in.1, f32[3,4096]{1,0:T(4,128)} %nrm_in.1, f32[32,128]{1,0:T(8,128)} %bitcast.7, f32[3,4096]{1,0:T(4,128)} %dsp_in.1, s32[2,160]{1,0:T(2,128)} %pair_in.1, s32[1]{0:T(128)S(6)} %copy.13.count_in, f32[32,128]{1,0:T(8,128)} %bitcast.8, ...), custom_call_target="tpu_custom_call" | custom-call | tf_op jit(solution)/shard_map/network/pallas_call | solution.py:530
  56.0 1.5 %deliver.1 = (f32[3,4096]{1,0:T(4,128)}, f32[32,128]{1,0:T(8,128)}, f32[32,128]{1,0:T(8,128)}) custom-call(f32[3,4096]{1,0:T(4,128)} %get-tuple-element.9.traction_in, f32[32,128]{1,0:T(8,128)} %get-tuple-element.10.pressure_in, f32[32,128]{1,0:T(8,128)} %get-tuple-element.11.residual_in), custom_call_target="tpu_custom_call" | custom-call | tf_op jit(solution)/shard_map/deliver/pallas_call | solution.py:552

commit v3 on v2

--- a/solution.py
+++ b/solution.py
@@ -52,14 +52,13 @@
     pairs,
     pair_rows,
     count,
-    base,
-    sto,
-    off,
+    bases,
+    stores,
+    offs,
     prev_pos,
     prev_nrm,
     prev_scl,
     prev_dsp,
-    base_next,
     table_inj,
     tfeat,
     sfeat,
@@ -70,8 +69,10 @@
     con_s,
     near0,
     near12,
-    got0,
-    got0_far,
+    got_prev,
+    got_next,
+    got_next2,
+    got_next3,
     got12,
     onehot,
     lanes_hot,
@@ -80,10 +81,6 @@
     table,
     landed_out,
     landed_in,
-    part_out,
-    part_in,
-    landed2_out,
-    landed2_in,
     sums_out,
     sums_near,
     sums_far,
@@ -119,7 +116,7 @@
         )
 
     groups = (core_size * low_size, x_size * high_size)
-    mates = [device(shift) for shift in (1, -1, 2, -2)]
+    mates = [device(shift) for shift in (1, -1, 2, -2, 3, -3)]
     mates += [mate(stage, j) for stage in (0, 1) for j in range(1, groups[stage])]
     barrier = pltpu.get_barrier_semaphore()
     for to in mates:
@@ -134,10 +131,10 @@
             (pair_in, pairs),
             (pair_in, pair_rows),
             (count_in, count),
-            (inj_in, table_inj.at[pl.ds(0, NB)]),
-            (off_in, off),
-            (base_in, base),
-            (sto_in, sto),
+            (inj_in, table_inj.at[pl.ds(NB, NB)]),
+            (off_in, offs.at[1]),
+            (base_in, bases.at[1]),
+            (sto_in, stores.at[0]),
         )
     ):
         loads[slot] = pltpu.make_async_copy(src, dst, load_sem.at[slot])
@@ -156,7 +153,7 @@
         copy.start()
         return copy
 
-    after, before, before2 = device(1), device(-1), device(-2)
+    after, before, before2, before3 = (device(shift) for shift in (1, -1, -2, -3))
     frame = [
         send(pos_in, prev_pos, 0, after),
         send(nrm_in, prev_nrm, 1, after),
@@ -164,10 +161,13 @@
         send(dsp_in, prev_dsp, 3, after),
     ]
     early = [
-        send(base_in, base_next, 4, before),
-        send(inj_in, table_inj.at[pl.ds(NB, NB)], 5, before),
+        send(inj_in, table_inj.at[pl.ds(2 * NB, NB)], 4, before),
+        send(off_in, offs.at[2], 5, before),
+        send(base_in, bases.at[2], 6, before),
+        send(sto_in, stores.at[1], 7, before),
+        send(inj_in, table_inj.at[pl.ds(3 * NB, NB)], 8, before2),
+        send(base_in, bases.at[3], 9, before2),
     ]
-
     for load in loads.values():
         load.wait()
 
@@ -248,51 +248,6 @@
     onehot[0] = jnp.where(live & (block == tgt), 1.0, 0.0).astype(BF16)
     onehot[1] = jnp.where(live & (block == src) & (src != tgt), 1.0, 0.0).astype(BF16)
 
-    element = (
-        lax.broadcasted_iota(jnp.int32, (NB, BLK), 0) * BLK
-        + lax.broadcasted_iota(jnp.int32, (NB, BLK), 1)
-    )
-    partner = element + off[...]
-    part_row = partner >> 7
-    part_lane = partner & 127
-    inside = jnp.where((me < devices - 1) | (partner < NB * BLK), 0.5, 0.0).astype(F32)
-    iota_lane = lax.broadcasted_iota(jnp.int32, (BLK, BLK), 1).astype(F32)
-    iota_row = lax.broadcasted_iota(jnp.int32, (2 * NB, BLK), 0)
-    upright_lane = part_lane.astype(F32).T
-    for k in range(NB):
-        lane = pl.ds(k * BLK, BLK)
-        lanes_hot[lane, :] = jnp.where(iota_lane == upright_lane[:, k : k + 1], 1.0, 0.0).astype(BF16)
-        rows_hot[:, lane] = jnp.where(iota_row == part_row[k : k + 1], 1.0, 0.0).astype(BF16)
-
-    def gather(ref):
-        out = []
-        for v in range(NB // 8):
-            lane = part_lane[8 * v : 8 * v + 8]
-            hot = part_row[8 * v : 8 * v + 8]
-            acc = jnp.zeros((8, BLK), F32)
-            for h in range(8 * v, 8 * v + 8 + NB):
-                line = jnp.broadcast_to(ref[h : h + 1, :], (8, BLK))
-                got = jnp.take_along_axis(line, lane, axis=1, mode="promise_in_bounds")
-                acc = jnp.where(hot == h, got, acc)
-            out.append(acc)
-        return jnp.concatenate(out, 0)
-
-    def scatter(flux):
-        top, rest = split(flux, 2)
-        for k in range(NB):
-            lane = pl.ds(k * BLK, BLK)
-            hot = rows_hot[:, lane]
-            for first, x in ((0, top), (2 * NB, rest)):
-                line = jnp.broadcast_to(x[k : k + 1], (16, BLK)).astype(BF16)
-                spread[first : first + 2 * NB, lane] = hot * jnp.concatenate([line] * 4, 0)
-        both = jnp.dot(spread[...], lanes_hot[...], preferred_element_type=F32)
-        return both[: 2 * NB] + both[2 * NB :]
-
-    vec = table_inj[:NB, :]
-    for copy in early:
-        copy.wait_recv()
-    vec_diff = vec - gather(table_inj)
-
     def apply(i, u):
         s = pairs[1, i * UNROLL + u]
         out = lax.dot_general(dfeat[s], held[u], NT, preferred_element_type=F32)
@@ -324,6 +279,11 @@
     lax.fori_loop(1, NB // UNROLL, steps, 0)
     for copy in frame:
         copy.wait_recv()
+    early += [
+        send(inj_in, table_inj.at[pl.ds(0, NB)], 10, after),
+        send(off_in, offs.at[0], 11, after),
+        send(base_in, bases.at[0], 12, after),
+    ]
     lax.fori_loop(
         0, NB, functools.partial(source_block, prev_pos, prev_nrm, prev_scl, prev_dsp, 0, me > 0), 0
     )
@@ -341,11 +301,78 @@
 
     first = blocks((0,))
     near0[...] = first
-    move0 = [send(near0, got0, 6, before), send(near0.at[pl.ds(0, NB)], got0_far, 7, before2)]
+    move0 = [
+        send(near0.at[pl.ds(0, NB)], got_next3, 13, before3),
+        send(near0, got_next2, 14, before2),
+        send(near0, got_next, 15, before),
+        send(near0.at[pl.ds(NB, NB)], got_prev, 16, after),
+    ]
     others = blocks((1, 2))
     near12[0] = others[:NB, :BLK]
     near12[1] = others[:NB, BLK:]
-    move12 = send(near12, got12, 8, before)
+    move12 = send(near12, got12, 17, before)
+
+    element = (
+        lax.broadcasted_iota(jnp.int32, (NB, BLK), 0) * BLK
+        + lax.broadcasted_iota(jnp.int32, (NB, BLK), 1)
+    )
+    iota_lane = lax.broadcasted_iota(jnp.int32, (BLK, BLK), 1).astype(F32)
+    hot_first = (0, NB, 3 * NB)
+    hot_rows = ((NB, 2 * NB), (0, 2 * NB), (0, NB))
+    part_row, part_lane, inside = [], [], []
+    for copy in early:
+        copy.wait_recv()
+    for e in range(3):
+        partner = element + offs[e]
+        part_row.append(partner >> 7)
+        part_lane.append(partner & 127)
+        if e == 0:
+            kept = me > 0
+        else:
+            kept = (me < devices - e) | (partner < NB * BLK)
+        inside.append(jnp.where(kept, 0.5, 0.0).astype(F32))
+        begin, end = hot_rows[e]
+        iota_row = lax.broadcasted_iota(jnp.int32, (end - begin, BLK), 0) + begin
+        upright_lane = part_lane[e].astype(F32).T
+        for k in range(NB):
+            lane = pl.ds(k * BLK, BLK)
+            lanes_hot[e, lane, :] = jnp.where(
+                iota_lane == upright_lane[:, k : k + 1], 1.0, 0.0
+            ).astype(BF16)
+            rows_hot[hot_first[e] : hot_first[e] + end - begin, lane] = jnp.where(
+                iota_row == part_row[e][k : k + 1], 1.0, 0.0
+            ).astype(BF16)
+
+    def gather(ref, e):
+        out = []
+        for v in range(NB // 8):
+            lane = part_lane[e][8 * v : 8 * v + 8]
+            hot = part_row[e][8 * v : 8 * v + 8]
+            acc = jnp.zeros((8, BLK), F32)
+            for h in range(8 * v, 8 * v + 8 + NB):
+                line = jnp.broadcast_to(ref[NB * e + h : NB * e + h + 1, :], (8, BLK))
+                got = jnp.take_along_axis(line, lane, axis=1, mode="promise_in_bounds")
+                acc = jnp.where(hot == h, got, acc)
+            out.append(acc)
+        return jnp.concatenate(out, 0)
+
+    def scatter(flux, e):
+        size = hot_rows[e][1] - hot_rows[e][0]
+        hot_at = hot_first[e]
+        at = 2 * hot_at
+        for k in range(NB):
+            lane = pl.ds(k * BLK, BLK)
+            hot = rows_hot[hot_at : hot_at + size, lane]
+            for first_row, x in zip((at, at + size), split(flux, 2)):
+                line = jnp.broadcast_to(x[k : k + 1], (16, BLK)).astype(BF16)
+                line = jnp.concatenate([line] * (size // 16), 0)
+                spread[first_row : first_row + size, lane] = hot * line
+        both = jnp.dot(spread[at : at + 2 * size, :], lanes_hot[e], preferred_element_type=F32)
+        return both[:size] + both[size:]
+
+    vecs = [table_inj[NB * e : NB * (e + 1), :] for e in range(3)]
+    diffs = [vecs[e] - gather(table_inj, e) for e in range(3)]
+    vec, sto = vecs[1], stores[0]
 
     def cubed(scale, t):
         aperture = scale * (1.0 + 0.5 * jnp.tanh(t))
@@ -353,30 +380,30 @@
 
     for copy in move0:
         copy.wait_recv()
-    traction0 = first[NB:] + got0[:NB, :]
-    cube = cubed(base[...], traction0)
-    table[:NB, :] = cube
-    table[NB:, :] = cubed(base_next[...], got0[NB:, :] + got0_far[...])
-    weight = inside * (cube + gather(table))
-
-    flux = weight * vec_diff
-    landed = scatter(flux)
-    part = sto[...] * vec + flux - landed[:NB]
-    landed_out[...] = landed[NB:]
-    part_out[...] = part
-    move_q = [send(landed_out, landed_in, 9, after), send(part_out, part_in, 10, before)]
-    for copy in move_q:
-        copy.wait_recv()
-    q = part - landed_in[...]
-    table[:NB, :] = q
-    table[NB:, :] = part_in[...] - landed[NB:]
-    q_diff = q - gather(table)
+    traction0 = first[NB:] + got_next[:NB, :]
+    cubes = [
+        cubed(bases[0], got_prev[...] + first[:NB]),
+        cubed(bases[1], traction0),
+        cubed(bases[2], got_next[NB:, :] + got_next2[:NB, :]),
+        cubed(bases[3], got_next2[NB:, :] + got_next3[...]),
+    ]
+    for e in range(4):
+        table[NB * e : NB * (e + 1), :] = cubes[e]
+    weights = [inside[e] * (cubes[e] + gather(table, e)) for e in range(3)]
+    weight = weights[1]
+    fluxes = [weights[e] * diffs[e] for e in range(3)]
+    landed = [scatter(fluxes[e], e) for e in range(3)]
+    q = sto * vec + fluxes[1] - landed[1][:NB] - landed[0]
+    q_next = stores[1] * vecs[2] + fluxes[2] - landed[2] - landed[1][NB:]
+    table[NB : 2 * NB, :] = q
+    table[2 * NB : 3 * NB, :] = q_next
+    q_diff = q - gather(table, 1)
     flux = weight * q_diff
 
     def line(x):
         return jnp.sum(x, axis=0, keepdims=True)
 
-    rows = [line(vec * vec), line(vec * q), line(q * q), line(sto[...] * q * q + flux * q_diff)]
+    rows = [line(vec * vec), line(vec * q), line(q * q), line(sto * q * q + flux * q_diff)]
     sums = jnp.concatenate(rows + [jnp.zeros((4, BLK), F32)], 0)
 
     def distance(stage, j):
@@ -408,10 +435,10 @@
         return parts[0]
 
     exchange(0, sums, sums_near)
-    landed = scatter(flux)
-    landed2_out[...] = landed[NB:]
-    move_u = send(landed2_out, landed2_in, 11, after)
-    u_part = sto[...] * q + flux - landed[:NB]
+    landed = scatter(flux, 1)
+    landed_out[...] = landed[NB:]
+    move_u = send(landed_out, landed_in, 18, after)
+    u_part = sto * q + flux - landed[:NB]
     sums = collect(0, sums, sums_near)
     exchange(1, sums, sums_far)
     move12.wait_recv()
@@ -424,7 +451,7 @@
         rows = [x[k : k + 1] for x in full]
         traction[:, pl.ds(k * BLK, BLK)] = jnp.concatenate(rows, 0)
     move_u.wait_recv()
-    u = u_part - landed2_in[...]
+    u = u_part - landed_in[...]
     sums = collect(1, sums, sums_far)
 
     total = jnp.sum(sums, axis=1, keepdims=True)
@@ -438,7 +465,7 @@
     residual[...] = r1 - alpha1 * (keep * q - alpha0 * u)
     pressure[...] = alpha0 * vec + alpha1 * (r1 + beta * vec)
 
-    for copy in frame + early + move0 + [move12] + move_q + [move_u]:
+    for copy in frame + early + move0 + [move12, move_u]:
         copy.wait_send()
     pltpu.make_async_copy(sums_near, sums_near, red_send.at[0]).wait()
     pltpu.make_async_copy(sums_far, sums_far, red_send.at[1]).wait()
@@ -473,23 +500,25 @@
     square = (NB, BLK)
     vmem = pl.BlockSpec(memory_space=pltpu.VMEM)
     anywhere = pl.BlockSpec(memory_space=pl.ANY)
+    rows3 = pltpu.VMEM((3, NB * BLK), F32)
+    tile = pltpu.VMEM(square, F32)
+    double = pltpu.VMEM((2 * NB, BLK), F32)
     scratch = [
-        pltpu.VMEM((3, NB * BLK), F32),
-        pltpu.VMEM((3, NB * BLK), F32),
-        pltpu.VMEM(square, F32),
-        pltpu.VMEM((3, NB * BLK), F32),
+        rows3,
+        rows3,
+        tile,
+        rows3,
         pltpu.SMEM((2, PMAX), jnp.int32),
         pltpu.VMEM((2, PMAX), jnp.int32),
         pltpu.SMEM((1,), jnp.int32),
-        pltpu.VMEM(square, F32),
-        pltpu.VMEM(square, F32),
-        pltpu.VMEM(square, jnp.int32),
-        pltpu.VMEM((3, NB * BLK), F32),
-        pltpu.VMEM((3, NB * BLK), F32),
-        pltpu.VMEM(square, F32),
-        pltpu.VMEM((3, NB * BLK), F32),
-        pltpu.VMEM(square, F32),
-        pltpu.VMEM((2 * NB, BLK), F32),
+        pltpu.VMEM((4, NB, BLK), F32),
+        pltpu.VMEM((2, NB, BLK), F32),
+        pltpu.VMEM((3, NB, BLK), jnp.int32),
+        rows3,
+        rows3,
+        tile,
+        rows3,
+        pltpu.VMEM((4 * NB, BLK), F32),
         pltpu.VMEM((NB, BLK, 48), BF16),
         pltpu.VMEM((2 * NB, 48, 2 * BLK), BF16),
         pltpu.VMEM((2 * NB, 16, 2 * BLK), BF16),
@@ -497,27 +526,25 @@
         pltpu.VMEM((UNROLL, BLK, 2 * BLK), BF16),
         pltpu.VMEM((3, PMAX // 8, 8, BLK), F32),
         pltpu.VMEM((3, PMAX // 8, 8, BLK), F32),
-        pltpu.VMEM((2 * NB, BLK), F32),
+        double,
         pltpu.VMEM((2, NB, BLK), F32),
-        pltpu.VMEM((2 * NB, BLK), F32),
-        pltpu.VMEM(square, F32),
+        tile,
+        double,
+        double,
+        tile,
         pltpu.VMEM((2, NB, BLK), F32),
         pltpu.VMEM((2, 2 * NB, PMAX), BF16),
-        pltpu.VMEM((NB * BLK, BLK), BF16),
-        pltpu.VMEM((2 * NB, NB * BLK), BF16),
+        pltpu.VMEM((3, NB * BLK, BLK), BF16),
         pltpu.VMEM((4 * NB, NB * BLK), BF16),
-        pltpu.VMEM((2 * NB, BLK), F32),
-        pltpu.VMEM(square, F32),
-        pltpu.VMEM(square, F32),
-        pltpu.VMEM(square, F32),
-        pltpu.VMEM(square, F32),
-        pltpu.VMEM(square, F32),
-        pltpu.VMEM(square, F32),
+        pltpu.VMEM((8 * NB, NB * BLK), BF16),
+        pltpu.VMEM((4 * NB, BLK), F32),
+        tile,
+        tile,
         pltpu.VMEM((2, 8, BLK), F32),
         pltpu.VMEM((2 * low_size - 1, 8, BLK), F32),
         pltpu.VMEM((grp_size // 2 * high_size - 1, 8, BLK), F32),
-        pltpu.SemaphoreType.DMA((12,)),
-        pltpu.SemaphoreType.DMA((12,)),
+        pltpu.SemaphoreType.DMA((19,)),
+        pltpu.SemaphoreType.DMA((19,)),
         pltpu.SemaphoreType.DMA((2,)),
         pltpu.SemaphoreType.DMA((2,)),
         pltpu.SemaphoreType.DMA((11,)),

time: 57.7 us -> 56.3 us (0.976)
  Pallas kernels: 56.2 us -> 54.8 us
    pallas_call x1, Pallas kernels: 54.7 us -> 53.3 us  [shards(): pl.pallas_call(functools.partial(kernel, sizes), out_shape=shapes, in_spe...]
where the time goes in v3:
time: 56.3 us; the launch traced here: 56.1 us
  Pallas kernels  54.8 us (97%)
  between operations  1.29 us (2%)
    pallas_call x1, Pallas kernels, shards(): pl.pallas_call(functools.partial(kernel, sizes), out_shape=shapes, in_spe...  53.3 us
    pallas_call x1, Pallas kernels, shards(): pl.pallas_call(deliver, out_shape=shapes, in_specs=[vmem] * 3, out_specs=...  1.52 us

profile of v3, /device:TPU:1, one launch (start us, length us, event | category | flops | bytes accessed | tf_op | source)
XLA Modules:
  0.0 56.1 jit_solution(10375713731829164992)
XLA Ops:
  1.3 53.3 %network.1 = (f32[3,4096]{1,0:T(4,128)}, f32[32,128]{1,0:T(8,128)}, f32[32,128]{1,0:T(8,128)}) custom-call(f32[3,4096]{1,0:T(4,128)} %pos_in.1, f32[3,4096]{1,0:T(4,128)} %nrm_in.1, f32[32,128]{1,0:T(8,128)} %bitcast.7, f32[3,4096]{1,0:T(4,128)} %dsp_in.1, s32[2,160]{1,0:T(2,128)} %pair_in.1, s32[1]{0:T(128)S(6)} %copy.13.count_in, f32[32,128]{1,0:T(8,128)} %bitcast.8, ...), custom_call_target="tpu_custom_call" | custom-call | tf_op jit(solution)/shard_map/network/pallas_call | solution.py:557
  54.5 1.5 %deliver.1 = (f32[3,4096]{1,0:T(4,128)}, f32[32,128]{1,0:T(8,128)}, f32[32,128]{1,0:T(8,128)}) custom-call(f32[3,4096]{1,0:T(4,128)} %get-tuple-element.9.traction_in, f32[32,128]{1,0:T(8,128)} %get-tuple-element.10.pressure_in, f32[32,128]{1,0:T(8,128)} %get-tuple-element.11.residual_in), custom_call_target="tpu_custom_call" | custom-call | tf_op jit(solution)/shard_map/deliver/pallas_call | solution.py:579

commit v4 on v3

--- a/solution.py
+++ b/solution.py
@@ -168,8 +168,8 @@
         send(inj_in, table_inj.at[pl.ds(3 * NB, NB)], 8, before2),
         send(base_in, bases.at[3], 9, before2),
     ]
-    for load in loads.values():
-        load.wait()
+    for slot in range(4):
+        loads[slot].wait()
 
     row = lax.broadcasted_iota(jnp.int32, (8, BLK), 0)
     low4 = row < 4
@@ -179,7 +179,7 @@
     zeros8 = jnp.zeros((8, BLK), F32)
     centre = jnp.mean(pos[...], axis=1, keepdims=True)
 
-    def target_block(k, _):
+    def target_block(k):
         lane = pl.ds(pl.multiple_of(k * BLK, BLK), BLK)
         p = pos[:, lane] - centre
         q = quads(p, jnp.sum(p * p, axis=0, keepdims=True))
@@ -197,14 +197,12 @@
         ]
         d = dsp[:, lane]
         rows += [jnp.concatenate([d, jnp.zeros((5, BLK), F32)], 0)]
-        rows += [zeros8] * 9
         upright = jnp.concatenate(rows, 0).T
         tfeat[k] = upright[:, :48].astype(BF16)
         for c in range(3):
             columns[k, c] = jnp.broadcast_to(upright[:, 48 + c : 49 + c], (BLK, BLK))
-        return 0
-
-    def source_block(pos_ref, nrm_ref, scl_ref, dsp_ref, first, factor, k, _):
+
+    def source_block(pos_ref, nrm_ref, scl_ref, dsp_ref, first, factor, k):
         lane = pl.ds(pl.multiple_of(k * BLK, BLK), BLK)
         p = pos_ref[:, lane] - centre
         q1, q2, q3 = split(quads(p, jnp.sum(p * p, axis=0, keepdims=True) + 0.25), 3)
@@ -235,10 +233,22 @@
         both = jnp.concatenate([jnp.where(low4, d1, d2), zeros8], 0).astype(BF16)
         dfeat[first + k, :, :BLK] = both
         dfeat[first + k, :, BLK:] = both
+
+    def own_blocks(i, _):
+        for j in range(4):
+            target_block(4 * i + j)
+            source_block(pos, nrm, scl, dsp, NB, None, 4 * i + j)
         return 0
 
-    lax.fori_loop(0, NB, target_block, 0)
-    lax.fori_loop(0, NB, functools.partial(source_block, pos, nrm, scl, dsp, NB, None), 0)
+    def prev_blocks(i, _):
+        for j in range(8):
+            source_block(prev_pos, prev_nrm, prev_scl, prev_dsp, 0, me > 0, 8 * i + j)
+        return 0
+
+    lax.fori_loop(0, NB // 4, own_blocks, 0)
+
+    for slot in range(4, 11):
+        loads[slot].wait()
 
     slot = lax.broadcasted_iota(jnp.int32, (2 * NB, PMAX), 1)
     block = lax.broadcasted_iota(jnp.int32, (2 * NB, PMAX), 0)
@@ -284,9 +294,7 @@
         send(off_in, offs.at[0], 11, after),
         send(base_in, bases.at[0], 12, after),
     ]
-    lax.fori_loop(
-        0, NB, functools.partial(source_block, prev_pos, prev_nrm, prev_scl, prev_dsp, 0, me > 0), 0
-    )
+    lax.fori_loop(0, NB // 8, prev_blocks, 0)
     lax.fori_loop(NB // UNROLL, PMAX // UNROLL, steps, 0)
     for u in range(UNROLL):
         apply(PMAX // UNROLL - 1, u)
@@ -360,10 +368,11 @@
         size = hot_rows[e][1] - hot_rows[e][0]
         hot_at = hot_first[e]
         at = 2 * hot_at
+        top, rest = split(flux, 2)
         for k in range(NB):
             lane = pl.ds(k * BLK, BLK)
             hot = rows_hot[hot_at : hot_at + size, lane]
-            for first_row, x in zip((at, at + size), split(flux, 2)):
+            for first_row, x in ((at, top), (at + size, rest)):
                 line = jnp.broadcast_to(x[k : k + 1], (16, BLK)).astype(BF16)
                 line = jnp.concatenate([line] * (size // 16), 0)
                 spread[first_row : first_row + size, lane] = hot * line

time: 56.3 us -> 51.9 us (0.922)
  Pallas kernels: 54.8 us -> 50.5 us
    pallas_call x1, Pallas kernels: 53.3 us -> 48.9 us  [shards(): pl.pallas_call(functools.partial(kernel, sizes), out_shape=shapes, in_spe...]
where the time goes in v4:
time: 51.9 us; the launch traced here: 51.7 us
  Pallas kernels  50.5 us (97%)
  between operations  1.29 us (2%)
    pallas_call x1, Pallas kernels, shards(): pl.pallas_call(functools.partial(kernel, sizes), out_shape=shapes, in_spe...  48.9 us
    pallas_call x1, Pallas kernels, shards(): pl.pallas_call(deliver, out_shape=shapes, in_specs=[vmem] * 3, out_specs=...  1.52 us

profile of v4, /device:TPU:1, one launch (start us, length us, event | category | flops | bytes accessed | tf_op | source)
XLA Modules:
  0.0 51.7 jit_solution(5494461470117962358)
XLA Ops:
  1.3 48.9 %network.1 = (f32[3,4096]{1,0:T(4,128)}, f32[32,128]{1,0:T(8,128)}, f32[32,128]{1,0:T(8,128)}) custom-call(f32[3,4096]{1,0:T(4,128)} %pos_in.1, f32[3,4096]{1,0:T(4,128)} %nrm_in.1, f32[32,128]{1,0:T(8,128)} %bitcast.7, f32[3,4096]{1,0:T(4,128)} %dsp_in.1, s32[2,160]{1,0:T(2,128)} %pair_in.1, s32[1]{0:T(128)S(6)} %copy.13.count_in, f32[32,128]{1,0:T(8,128)} %bitcast.8, ...), custom_call_target="tpu_custom_call" | custom-call | tf_op jit(solution)/shard_map/network/pallas_call | solution.py:566
  50.2 1.5 %deliver.1 = (f32[3,4096]{1,0:T(4,128)}, f32[32,128]{1,0:T(8,128)}, f32[32,128]{1,0:T(8,128)}) custom-call(f32[3,4096]{1,0:T(4,128)} %get-tuple-element.9.traction_in, f32[32,128]{1,0:T(8,128)} %get-tuple-element.10.pressure_in, f32[32,128]{1,0:T(8,128)} %get-tuple-element.11.residual_in), custom_call_target="tpu_custom_call" | custom-call | tf_op jit(solution)/shard_map/deliver/pallas_call | solution.py:588

commit v5 on v4

--- a/solution.py
+++ b/solution.py
@@ -107,38 +107,57 @@
             digit = lax.rem(digit, size)
         return index + (lax.rem(digit + shift, size) - digit) * low
 
+    groups = (core_size * low_size, x_size * high_size)
+    rings = (
+        (
+            [ring(grp, core_size, 1, j) for j in range(core_size)],
+            [ring(seg, low_size, 1, j) for j in range(low_size)],
+        ),
+        (
+            [ring(grp, x_size, core_size, j) for j in range(x_size)],
+            [ring(seg, high_size, low_size, j) for j in range(high_size)],
+        ),
+    )
+
     def mate(stage, j):
-        if stage == 0:
-            return (ring(grp, core_size, 1, j % core_size), ring(seg, low_size, 1, j // core_size))
-        return (
-            ring(grp, x_size, core_size, j % x_size),
-            ring(seg, high_size, low_size, j // x_size),
-        )
-
-    groups = (core_size * low_size, x_size * high_size)
-    mates = [device(shift) for shift in (1, -1, 2, -2, 3, -3)]
-    mates += [mate(stage, j) for stage in (0, 1) for j in range(1, groups[stage])]
+        narrow, wide = rings[stage]
+        return (narrow[j % len(narrow)], wide[j // len(narrow)])
+
+    def distance(stage, j):
+        narrow, wide = (len(x) for x in rings[stage])
+        near, far = j % narrow, j // narrow
+        return min(far, wide - far) + min(near, narrow - near)
+
+    orders = [
+        sorted(range(1, groups[stage]), key=functools.partial(distance, stage))[::-1]
+        for stage in (0, 1)
+    ]
+
+    def start_load(slot, src, dst):
+        load = pltpu.make_async_copy(src, dst, load_sem.at[slot])
+        load.start()
+        return load
+
+    loads = [
+        start_load(0, pos_in, pos),
+        start_load(1, nrm_in, nrm),
+        start_load(2, scl_in, scl),
+        start_load(3, dsp_in, dsp),
+    ]
+    mates = [mate(stage, j) for stage in (1, 0) for j in orders[stage]]
+    mates += [device(shift) for shift in (3, -3, 2, -2, 1, -1)]
     barrier = pltpu.get_barrier_semaphore()
     for to in mates:
         pl.semaphore_signal(barrier, inc=1, device_id=to, device_id_type=MESH)
-    loads = {}
-    for slot, (src, dst) in enumerate(
-        (
-            (pos_in, pos),
-            (nrm_in, nrm),
-            (scl_in, scl),
-            (dsp_in, dsp),
-            (pair_in, pairs),
-            (pair_in, pair_rows),
-            (count_in, count),
-            (inj_in, table_inj.at[pl.ds(NB, NB)]),
-            (off_in, offs.at[1]),
-            (base_in, bases.at[1]),
-            (sto_in, stores.at[0]),
-        )
-    ):
-        loads[slot] = pltpu.make_async_copy(src, dst, load_sem.at[slot])
-        loads[slot].start()
+    loads += [
+        start_load(4, pair_in, pairs),
+        start_load(5, pair_in, pair_rows),
+        start_load(6, count_in, count),
+        start_load(7, inj_in, table_inj.at[pl.ds(NB, NB)]),
+        start_load(8, off_in, offs.at[1]),
+        start_load(9, base_in, bases.at[1]),
+        start_load(10, sto_in, stores.at[0]),
+    ]
     pl.semaphore_wait(barrier, len(mates))
 
     def send(src, dst, slot, to):
@@ -202,7 +221,7 @@
         for c in range(3):
             columns[k, c] = jnp.broadcast_to(upright[:, 48 + c : 49 + c], (BLK, BLK))
 
-    def source_block(pos_ref, nrm_ref, scl_ref, dsp_ref, first, factor, k):
+    def source_block(pos_ref, nrm_ref, scl_ref, first, factor, k):
         lane = pl.ds(pl.multiple_of(k * BLK, BLK), BLK)
         p = pos_ref[:, lane] - centre
         q1, q2, q3 = split(quads(p, jnp.sum(p * p, axis=0, keepdims=True) + 0.25), 3)
@@ -228,6 +247,9 @@
         ]
         sfeat[first + k, :, :BLK] = jnp.concatenate(ahead, 0).astype(BF16)
         sfeat[first + k, :, BLK:] = jnp.concatenate(align, 0).astype(BF16)
+
+    def moved_block(dsp_ref, first, k):
+        lane = pl.ds(pl.multiple_of(k * BLK, BLK), BLK)
         d = dsp_ref[:, lane]
         d1, d2 = split(quads(d, jnp.zeros((1, BLK), F32)), 2)
         both = jnp.concatenate([jnp.where(low4, d1, d2), zeros8], 0).astype(BF16)
@@ -237,12 +259,18 @@
     def own_blocks(i, _):
         for j in range(4):
             target_block(4 * i + j)
-            source_block(pos, nrm, scl, dsp, NB, None, 4 * i + j)
+            source_block(pos, nrm, scl, NB, None, 4 * i + j)
+            moved_block(dsp, NB, 4 * i + j)
         return 0
 
     def prev_blocks(i, _):
         for j in range(8):
-            source_block(prev_pos, prev_nrm, prev_scl, prev_dsp, 0, me > 0, 8 * i + j)
+            source_block(prev_pos, prev_nrm, prev_scl, 0, me > 0, 8 * i + j)
+        return 0
+
+    def prev_moved(i, _):
+        for j in range(8):
+            moved_block(prev_dsp, 0, 8 * i + j)
         return 0
 
     lax.fori_loop(0, NB // 4, own_blocks, 0)
@@ -287,7 +315,7 @@
     for u in range(UNROLL):
         evaluate(0, u)
     lax.fori_loop(1, NB // UNROLL, steps, 0)
-    for copy in frame:
+    for copy in frame[:3]:
         copy.wait_recv()
     early += [
         send(inj_in, table_inj.at[pl.ds(0, NB)], 10, after),
@@ -295,6 +323,8 @@
         send(base_in, bases.at[0], 12, after),
     ]
     lax.fori_loop(0, NB // 8, prev_blocks, 0)
+    frame[3].wait_recv()
+    lax.fori_loop(0, NB // 8, prev_moved, 0)
     lax.fori_loop(NB // UNROLL, PMAX // UNROLL, steps, 0)
     for u in range(UNROLL):
         apply(PMAX // UNROLL - 1, u)
@@ -357,7 +387,7 @@
             lane = part_lane[e][8 * v : 8 * v + 8]
             hot = part_row[e][8 * v : 8 * v + 8]
             acc = jnp.zeros((8, BLK), F32)
-            for h in range(8 * v, 8 * v + 8 + NB):
+            for h in range(max(8 * v, hot_rows[e][0]), 8 * v + 8 + NB):
                 line = jnp.broadcast_to(ref[NB * e + h : NB * e + h + 1, :], (8, BLK))
                 got = jnp.take_along_axis(line, lane, axis=1, mode="promise_in_bounds")
                 acc = jnp.where(hot == h, got, acc)
@@ -415,18 +445,9 @@
     rows = [line(vec * vec), line(vec * q), line(q * q), line(sto * q * q + flux * q_diff)]
     sums = jnp.concatenate(rows + [jnp.zeros((4, BLK), F32)], 0)
 
-    def distance(stage, j):
-        if stage == 0:
-            wide, narrow, far = low_size, core_size, j // core_size
-        else:
-            wide, narrow, far = high_size, x_size, j // x_size
-        near = j % narrow
-        return min(far, wide - far) + min(near, narrow - near)
-
     def exchange(stage, sums, got):
         sums_out[stage] = sums
-        order = sorted(range(1, groups[stage]), key=functools.partial(distance, stage))
-        for j in order[::-1]:
+        for j in orders[stage]:
             pltpu.make_async_remote_copy(
                 src_ref=sums_out.at[stage],
                 dst_ref=got.at[j - 1],

time: 51.9 us -> 51.3 us (0.988)
  Pallas kernels: 50.5 us -> 49.8 us
    pallas_call x1, Pallas kernels: 48.9 us -> 48.3 us  [shards(): pl.pallas_call(functools.partial(kernel, sizes), out_shape=shapes, in_spe...]
where the time goes in v5:
time: 51.3 us; the launch traced here: 51.1 us
  Pallas kernels  49.8 us (97%)
  between operations  1.29 us (3%)
    pallas_call x1, Pallas kernels, shards(): pl.pallas_call(functools.partial(kernel, sizes), out_shape=shapes, in_spe...  48.3 us
    pallas_call x1, Pallas kernels, shards(): pl.pallas_call(deliver, out_shape=shapes, in_specs=[vmem] * 3, out_specs=...  1.52 us

profile of v5, /device:TPU:1, one launch (start us, length us, event | category | flops | bytes accessed | tf_op | source)
XLA Modules:
  0.0 51.1 jit_solution(14487151815389646879)
XLA Ops:
  1.3 48.3 %network.1 = (f32[3,4096]{1,0:T(4,128)}, f32[32,128]{1,0:T(8,128)}, f32[32,128]{1,0:T(8,128)}) custom-call(f32[3,4096]{1,0:T(4,128)} %pos_in.1, f32[3,4096]{1,0:T(4,128)} %nrm_in.1, f32[32,128]{1,0:T(8,128)} %bitcast.7, f32[3,4096]{1,0:T(4,128)} %dsp_in.1, s32[2,160]{1,0:T(2,128)} %pair_in.1, s32[1]{0:T(128)S(6)} %copy.13.count_in, f32[32,128]{1,0:T(8,128)} %bitcast.8, ...), custom_call_target="tpu_custom_call" | custom-call | tf_op jit(solution)/shard_map/network/pallas_call | solution.py:587
  49.6 1.5 %deliver.1 = (f32[3,4096]{1,0:T(4,128)}, f32[32,128]{1,0:T(8,128)}, f32[32,128]{1,0:T(8,128)}) custom-call(f32[3,4096]{1,0:T(4,128)} %get-tuple-element.9.traction_in, f32[32,128]{1,0:T(8,128)} %get-tuple-element.10.pressure_in, f32[32,128]{1,0:T(8,128)} %get-tuple-element.11.residual_in), custom_call_target="tpu_custom_call" | custom-call | tf_op jit(solution)/shard_map/deliver/pallas_call | solution.py:609

commit v6 on v5

--- a/solution.py
+++ b/solution.py
@@ -14,7 +14,7 @@
 BF16 = jnp.bfloat16
 MESH = pl.DeviceIdType.MESH
 NT = (((1,), (1,)), ((), ()))
-UNROLL = 16
+UNROLL = 32
 
 
 def split(x, parts):
@@ -173,12 +173,18 @@
         return copy
 
     after, before, before2, before3 = (device(shift) for shift in (1, -1, -2, -3))
-    frame = [
-        send(pos_in, prev_pos, 0, after),
-        send(nrm_in, prev_nrm, 1, after),
-        send(scl_in, prev_scl, 2, after),
-        send(dsp_in, prev_dsp, 3, after),
-    ]
+    frame = []
+    for c in range(4):
+        lanes = pl.ds(c * (NB // 4) * BLK, NB // 4 * BLK)
+        rows = pl.ds(c * (NB // 4), NB // 4)
+        frame.append(
+            [
+                send(pos_in.at[:, lanes], prev_pos.at[:, lanes], 19 + 3 * c, after),
+                send(nrm_in.at[:, lanes], prev_nrm.at[:, lanes], 20 + 3 * c, after),
+                send(scl_in.at[rows], prev_scl.at[rows], 21 + 3 * c, after),
+            ]
+        )
+    frame_dsp = send(dsp_in, prev_dsp, 3, after)
     early = [
         send(inj_in, table_inj.at[pl.ds(2 * NB, NB)], 4, before),
         send(off_in, offs.at[2], 5, before),
@@ -263,11 +269,6 @@
             moved_block(dsp, NB, 4 * i + j)
         return 0
 
-    def prev_blocks(i, _):
-        for j in range(8):
-            source_block(prev_pos, prev_nrm, prev_scl, 0, me > 0, 8 * i + j)
-        return 0
-
     def prev_moved(i, _):
         for j in range(8):
             moved_block(prev_dsp, 0, 8 * i + j)
@@ -315,17 +316,20 @@
     for u in range(UNROLL):
         evaluate(0, u)
     lax.fori_loop(1, NB // UNROLL, steps, 0)
-    for copy in frame[:3]:
-        copy.wait_recv()
+    for c in range(4):
+        for copy in frame[c]:
+            copy.wait_recv()
+        for j in range(NB // 4):
+            source_block(prev_pos, prev_nrm, prev_scl, 0, me > 0, c * (NB // 4) + j)
     early += [
         send(inj_in, table_inj.at[pl.ds(0, NB)], 10, after),
         send(off_in, offs.at[0], 11, after),
         send(base_in, bases.at[0], 12, after),
     ]
-    lax.fori_loop(0, NB // 8, prev_blocks, 0)
-    frame[3].wait_recv()
+    lax.fori_loop(NB // UNROLL, NB // UNROLL + 1, steps, 0)
+    frame_dsp.wait_recv()
     lax.fori_loop(0, NB // 8, prev_moved, 0)
-    lax.fori_loop(NB // UNROLL, PMAX // UNROLL, steps, 0)
+    lax.fori_loop(NB // UNROLL + 1, PMAX // UNROLL, steps, 0)
     for u in range(UNROLL):
         apply(PMAX // UNROLL - 1, u)
 
@@ -417,21 +421,28 @@
         aperture = scale * (1.0 + 0.5 * jnp.tanh(t))
         return aperture * aperture * aperture
 
-    for copy in move0:
-        copy.wait_recv()
+    move0[3].wait_recv()
+    move0[2].wait_recv()
     traction0 = first[NB:] + got_next[:NB, :]
     cubes = [
         cubed(bases[0], got_prev[...] + first[:NB]),
         cubed(bases[1], traction0),
-        cubed(bases[2], got_next[NB:, :] + got_next2[:NB, :]),
-        cubed(bases[3], got_next2[NB:, :] + got_next3[...]),
-    ]
-    for e in range(4):
-        table[NB * e : NB * (e + 1), :] = cubes[e]
-    weights = [inside[e] * (cubes[e] + gather(table, e)) for e in range(3)]
+    ]
+    table[:NB, :] = cubes[0]
+    table[NB : 2 * NB, :] = cubes[1]
+    weights, fluxes, landed = [], [], []
+    for e in range(3):
+        if e == 1:
+            move0[1].wait_recv()
+            cubes.append(cubed(bases[2], got_next[NB:, :] + got_next2[:NB, :]))
+            table[2 * NB : 3 * NB, :] = cubes[2]
+        if e == 2:
+            move0[0].wait_recv()
+            table[3 * NB :, :] = cubed(bases[3], got_next2[NB:, :] + got_next3[...])
+        weights.append(inside[e] * (cubes[e] + gather(table, e)))
+        fluxes.append(weights[e] * diffs[e])
+        landed.append(scatter(fluxes[e], e))
     weight = weights[1]
-    fluxes = [weights[e] * diffs[e] for e in range(3)]
-    landed = [scatter(fluxes[e], e) for e in range(3)]
     q = sto * vec + fluxes[1] - landed[1][:NB] - landed[0]
     q_next = stores[1] * vecs[2] + fluxes[2] - landed[2] - landed[1][NB:]
     table[NB : 2 * NB, :] = q
@@ -495,7 +506,7 @@
     residual[...] = r1 - alpha1 * (keep * q - alpha0 * u)
     pressure[...] = alpha0 * vec + alpha1 * (r1 + beta * vec)
 
-    for copy in frame + early + move0 + [move12, move_u]:
+    for copy in sum(frame, [frame_dsp]) + early + move0 + [move12, move_u]:
         copy.wait_send()
     pltpu.make_async_copy(sums_near, sums_near, red_send.at[0]).wait()
     pltpu.make_async_copy(sums_far, sums_far, red_send.at[1]).wait()
@@ -573,8 +584,8 @@
         pltpu.VMEM((2, 8, BLK), F32),
         pltpu.VMEM((2 * low_size - 1, 8, BLK), F32),
         pltpu.VMEM((grp_size // 2 * high_size - 1, 8, BLK), F32),
-        pltpu.SemaphoreType.DMA((19,)),
-        pltpu.SemaphoreType.DMA((19,)),
+        pltpu.SemaphoreType.DMA((31,)),
+        pltpu.SemaphoreType.DMA((31,)),
         pltpu.SemaphoreType.DMA((2,)),
         pltpu.SemaphoreType.DMA((2,)),
         pltpu.SemaphoreType.DMA((11,)),

time: 51.3 us -> 50.8 us (level)
  no operation moved by 1% of the time
where the time goes in v6:
time: 50.8 us
  Pallas kernels  49.5 us (97%)
  between operations  1.29 us (3%)
    pallas_call x1, Pallas kernels, shards(): pl.pallas_call(functools.partial(kernel, sizes), out_shape=shapes, in_spe...  48 us
    pallas_call x1, Pallas kernels, shards(): pl.pallas_call(deliver, out_shape=shapes, in_specs=[vmem] * 3, out_specs=...  1.52 us

profile of v6, /device:TPU:1, one launch (start us, length us, event | category | flops | bytes accessed | tf_op | source)
XLA Modules:
  0.0 50.8 jit_solution(2159151007243129750)
XLA Ops:
  1.3 48.0 %network.1 = (f32[3,4096]{1,0:T(4,128)}, f32[32,128]{1,0:T(8,128)}, f32[32,128]{1,0:T(8,128)}) custom-call(f32[3,4096]{1,0:T(4,128)} %pos_in.1, f32[3,4096]{1,0:T(4,128)} %nrm_in.1, f32[32,128]{1,0:T(8,128)} %bitcast.7, f32[3,4096]{1,0:T(4,128)} %dsp_in.1, s32[2,160]{1,0:T(2,128)} %pair_in.1, s32[1]{0:T(128)S(6)} %copy.13.count_in, f32[32,128]{1,0:T(8,128)} %bitcast.8, ...), custom_call_target="tpu_custom_call" | custom-call | tf_op jit(solution)/shard_map/network/pallas_call | solution.py:598
  49.2 1.5 %deliver.1 = (f32[3,4096]{1,0:T(4,128)}, f32[32,128]{1,0:T(8,128)}, f32[32,128]{1,0:T(8,128)}) custom-call(f32[3,4096]{1,0:T(4,128)} %get-tuple-element.9.traction_in, f32[32,128]{1,0:T(8,128)} %get-tuple-element.10.pressure_in, f32[32,128]{1,0:T(8,128)} %get-tuple-element.11.residual_in), custom_call_target="tpu_custom_call" | custom-call | tf_op jit(solution)/shard_map/deliver/pallas_call | solution.py:620
